TPU v7x, 32 devices: a whole 2x2x4 slice. The times are simulated.
32 devices in a mesh: dp: 8 (over y, x, core), tm: 4 (over z).
Axes of the slice: x: 2, y: 2, z: 4, core: 2. Of those that a mesh axis runs over, the one named last changes fastest.
Arguments:
- inputs: bfloat16 [4, 8, 1536, 512], P(None, 'dp', 'tm'), may hold values from -6 to 6
- utterance_ids: int32 [4, 8, 1536], P(None, 'dp', 'tm'), may hold values from -1 to 3, as said below
- cotangent: bfloat16 [4, 8, 1536, 512], P(None, 'dp', 'tm'), may hold values from -6 to 6
- pointwise: float32 [6, 512, 512], P(None, ('dp', 'tm'))
- pointwise_first: float32 [6, 512, 512], P(None, ('dp', 'tm'))
- pointwise_second: float32 [6, 512, 512], P(None, ('dp', 'tm')), may hold values from 3072 to 12288
- depthwise: float32 [5, 5, 512], replicated, may hold values from -2.5 to 2.5
- depthwise_first: float32 [5, 5, 512], replicated
- depthwise_second: float32 [5, 5, 512], replicated, may hold values from 3072 to 12288
- norm_affine: float32 [2, 5, 512], replicated
- norm_first: float32 [2, 5, 512], replicated
- norm_second: float32 [2, 5, 512], replicated, may hold values from 3072 to 12288
- excite_mats: float32 [2, 64, 512], replicated
- excite_first: float32 [2, 64, 512], replicated
- excite_second: float32 [2, 64, 512], replicated, may hold values from 3072 to 12288
Outputs:
- block_out: bfloat16 [4, 8, 1536, 512], P(None, 'dp', 'tm')
- input_grad: float32 [4, 8, 1536, 512], P(None, 'dp', 'tm')
- pointwise_moment: float32 [6, 512, 512], P(None, ('dp', 'tm'))
- pointwise_square: float32 [6, 512, 512], P(None, ('dp', 'tm'))
- pointwise_new: float32 [6, 512, 512], P(None, ('dp', 'tm'))
- pointwise_half: bfloat16 [6, 512, 512], P(None, ('dp', 'tm'))
- depthwise_moment: float32 [5, 5, 512], replicated
- depthwise_square: float32 [5, 5, 512], replicated
- depthwise_new: float32 [5, 5, 512], replicated
- norm_moment: float32 [2, 5, 512], replicated
- norm_square: float32 [2, 5, 512], replicated
- norm_new: float32 [2, 5, 512], replicated
- excite_moment: float32 [2, 64, 512], replicated
- excite_square: float32 [2, 64, 512], replicated
- excite_new: float32 [2, 64, 512], replicated
- trust_norms: float32 [2, 23], replicated
Inputs may be any that keep to these rules, and one draw needn't show every extreme that they name: `utterance_ids`: -1 marks padding. Along a row the ids other than -1 never fall; every row holds each id 0 to 3 in one unbroken run of frames. In one row of each micro-batch, chosen by the seed, utterance 1 begins exactly at frame 1536 // 2.
All inputs are finite; a program needn't handle non-finite values.
Results may differ from a plain program's by a relative error of at most 0.024.
The roundings to bfloat16 on the way count: a program that leaves them out, or rounds other values in their place, can miss the bound.
Values may be sent and summed in bfloat16 or wider, within the bound.
No kernel may reach another device: no remote copies, remote signals or barrier semaphores. Data moves between devices by JAX's collectives and lax.ppermute only.
A program may use at most 192 MiB of HBM per device.

v0:
```python
import jax
import jax.numpy as jnp
from jax import lax
from jax.sharding import PartitionSpec as P

NSEG = 4
STEP = 5


HIGHEST = lax.Precision.HIGHEST
BN_EPS = 1e-05
BETA_ONE = 0.5
BETA_TWO = 0.5
LAMB_EPS = 1e-06
DECAY = 0.01
RATE = 1.0


def with_halo(block, sides, width):
    for axis, dim in sides:
        count = lax.axis_size(axis)
        forward = [(i, i + 1) for i in range(count - 1)]
        backward = [(target, source) for source, target in forward]
        low = lax.ppermute(
            lax.slice_in_dim(block, block.shape[dim] - width, None, axis=dim), axis, forward
        )
        high = lax.ppermute(lax.slice_in_dim(block, 0, width, axis=dim), axis, backward)
        block = jnp.concatenate([low, block, high], axis=dim)
    return block


def swish_act(value):
    return value * jax.nn.sigmoid(value)


def swish_slope(value):
    sigma = jax.nn.sigmoid(value)
    return sigma * (1.0 + value * (1.0 - sigma))


def depth_mix(padded, kernel, linked, frames):
    wide = padded.astype(jnp.float32)
    mixed = jnp.zeros((frames, padded.shape[1]), jnp.float32)
    for offset in range(kernel.shape[0]):
        mixed = mixed + kernel[offset] * wide[offset : offset + frames] * linked[offset][:, None]
    return mixed


def depth_back(grad_pad, kernel, linked, frames):
    wide = grad_pad.astype(jnp.float32)
    last = kernel.shape[0] - 1
    result = jnp.zeros((frames, grad_pad.shape[1]), jnp.float32)
    for offset in range(kernel.shape[0]):
        start = last - offset
        result = (
            result + kernel[offset] * wide[start : start + frames] * linked[last - offset][:, None]
        )
    return result


def depth_grad(grad_pad, padded, linked, frames, taps):
    center = grad_pad[2 : 2 + frames].astype(jnp.float32)
    wide = padded.astype(jnp.float32)
    return jnp.stack(
        [
            jnp.sum(center * wide[offset : offset + frames] * linked[offset][:, None], axis=0)
            for offset in range(taps)
        ]
    )


def lamb_terms(weights, first, second, grads):
    first_new = BETA_ONE * first + (1.0 - BETA_ONE) * grads
    second_new = BETA_TWO * second + (1.0 - BETA_TWO) * grads * grads
    first_hat = first_new / (1.0 - BETA_ONE**STEP)
    second_hat = second_new / (1.0 - BETA_TWO**STEP)
    update = first_hat / (jnp.sqrt(second_hat) + LAMB_EPS) + DECAY * weights
    return (first_new, second_new, update)


def local_lamb(weights, first, second, grads, axes):
    first_new, second_new, update = lamb_terms(weights, first, second, grads)
    weight_norm = jnp.sqrt(jnp.sum(weights * weights, axis=axes, keepdims=True))
    update_norm = jnp.sqrt(jnp.sum(update * update, axis=axes, keepdims=True))
    weights_new = weights - RATE * (weight_norm / update_norm) * update
    return (first_new, second_new, weights_new, weight_norm.reshape(-1), update_norm.reshape(-1))


def local(
    inputs,
    utterance_ids,
    cotangent,
    pointwise,
    pointwise_first,
    pointwise_second,
    depthwise,
    depthwise_first,
    depthwise_second,
    norm_affine,
    norm_first,
    norm_second,
    excite_mats,
    excite_first,
    excite_second,
):
    batches = inputs.shape[0]
    frames = inputs.shape[2]
    channels = inputs.shape[3]
    convs = depthwise.shape[0]
    taps = depthwise.shape[1]
    matrices = pointwise.shape[0]
    pointwise_low = pointwise.astype(jnp.bfloat16)
    excite_low = excite_mats.astype(jnp.bfloat16)
    segment_index = jnp.arange(NSEG, dtype=jnp.int32)
    tm_first = (lax.axis_index("tm") == 0).astype(jnp.float32)
    grad_point_acc = jnp.zeros((matrices, channels, channels), jnp.float32)
    grad_depth_acc = jnp.zeros(depthwise.shape, jnp.float32)
    grad_norm_acc = jnp.zeros(norm_affine.shape, jnp.float32)
    grad_excite_acc = jnp.zeros(excite_mats.shape, jnp.float32)
    outputs = []
    input_grads = []
    for batch_index in range(batches):
        batch_in = inputs[batch_index, 0]
        batch_ids = utterance_ids[batch_index, 0]
        batch_cot = cotangent[batch_index, 0].astype(jnp.float32)
        forward_weights = lax.all_gather(pointwise_low, ("dp", "tm"), axis=1, tiled=True)
        live_mask = (batch_ids >= 0).astype(jnp.float32)[:, None]
        ids_plus = batch_ids + 1
        ids_padded = with_halo(ids_plus, (("tm", 0),), 2)
        linked = jnp.stack(
            [
                ((ids_padded[offset : offset + frames] == ids_plus) & (batch_ids >= 0)).astype(
                    jnp.float32
                )
                for offset in range(taps)
            ]
        )
        hidden_low = batch_in
        hidden = None
        kept = []
        frame_total = None
        for layer in range(convs):
            if layer > 0:
                hidden_low = hidden.astype(jnp.bfloat16)
            padded = with_halo(hidden_low, (("tm", 0),), 2)
            mixed_low = depth_mix(padded, depthwise[layer], linked, frames).astype(jnp.bfloat16)
            point = jnp.dot(mixed_low, forward_weights[layer], preferred_element_type=jnp.float32)
            first_sum = jnp.sum(point * live_mask, axis=0)
            square_sum = jnp.sum(point * point * live_mask, axis=0)
            first_sum, square_sum, frame_total = lax.psum(
                (first_sum, square_sum, jnp.sum(live_mask)), ("dp", "tm")
            )
            average = first_sum / frame_total
            variance = square_sum / frame_total - average * average
            inv_std = lax.rsqrt(variance + BN_EPS)
            normed = (point - average) * inv_std
            affine = norm_affine[0, layer] * normed + norm_affine[1, layer]
            hidden = swish_act(affine) * live_mask
            kept.append((padded, mixed_low, normed, affine, inv_std))
        onehot = (batch_ids[:, None] == segment_index[None, :]).astype(jnp.float32)
        segment_sums = jnp.dot(onehot.T, hidden, precision=HIGHEST)
        segment_sums, frame_counts = lax.psum((segment_sums, jnp.sum(onehot, axis=0)), "tm")
        pooled_low = (segment_sums / frame_counts[:, None]).astype(jnp.bfloat16)
        squeeze = jnp.dot(pooled_low, excite_low[0].T, preferred_element_type=jnp.float32)
        squeeze_act = swish_act(squeeze).astype(jnp.bfloat16)
        excite = jnp.dot(squeeze_act, excite_low[1], preferred_element_type=jnp.float32)
        gating = jax.nn.sigmoid(excite)
        spread = jnp.dot(onehot, gating, precision=HIGHEST)
        residual = jnp.dot(batch_in, forward_weights[convs], preferred_element_type=jnp.float32)
        total = hidden * spread + residual
        outputs.append((swish_act(total) * live_mask).astype(jnp.bfloat16))
        backward_weights = lax.all_gather(pointwise_low, ("dp", "tm"), axis=1, tiled=True)
        grad_total = batch_cot * live_mask * swish_slope(total)
        grad_res_low = grad_total.astype(jnp.bfloat16)
        grad_input = jnp.dot(
            grad_res_low, backward_weights[convs].T, preferred_element_type=jnp.float32
        )
        grad_res_weight = jnp.dot(batch_in.T, grad_res_low, preferred_element_type=jnp.float32)
        grad_gating = lax.psum(jnp.dot(onehot.T, grad_total * hidden, precision=HIGHEST), "tm")
        grad_excite_low = (grad_gating * gating * (1.0 - gating)).astype(jnp.bfloat16)
        grad_upward = jnp.dot(squeeze_act.T, grad_excite_low, preferred_element_type=jnp.float32)
        grad_squeeze_act = jnp.dot(
            grad_excite_low, excite_low[1].T, preferred_element_type=jnp.float32
        )
        grad_squeeze_low = (grad_squeeze_act * swish_slope(squeeze)).astype(jnp.bfloat16)
        grad_down = jnp.dot(grad_squeeze_low.T, pooled_low, preferred_element_type=jnp.float32)
        grad_pooled = jnp.dot(grad_squeeze_low, excite_low[0], preferred_element_type=jnp.float32)
        grad_hidden = grad_total * spread + jnp.dot(
            onehot, grad_pooled / frame_counts[:, None], precision=HIGHEST
        )
        point_grads = [None] * convs
        depth_grads = [None] * convs
        gain_grads = [None] * convs
        shift_grads = [None] * convs
        for layer in reversed(range(convs)):
            padded, mixed_low, normed, affine, inv_std = kept[layer]
            grad_affine = grad_hidden * live_mask * swish_slope(affine)
            sum_grad = jnp.sum(grad_affine * live_mask, axis=0)
            sum_cross = jnp.sum(grad_affine * normed * live_mask, axis=0)
            sum_grad, sum_cross = lax.psum((sum_grad, sum_cross), ("dp", "tm"))
            gain_grads[layer] = sum_cross
            shift_grads[layer] = sum_grad
            grad_point_low = (
                live_mask
                * norm_affine[0, layer]
                * inv_std
                * (grad_affine - sum_grad / frame_total - normed * sum_cross / frame_total)
            ).astype(jnp.bfloat16)
            point_grads[layer] = jnp.dot(
                mixed_low.T, grad_point_low, preferred_element_type=jnp.float32
            )
            grad_mixed_low = jnp.dot(
                grad_point_low, backward_weights[layer].T, preferred_element_type=jnp.float32
            ).astype(jnp.bfloat16)
            grad_padded = with_halo(grad_mixed_low, (("tm", 0),), 2)
            depth_grads[layer] = depth_grad(grad_padded, padded, linked, frames, taps)
            grad_hidden = depth_back(grad_padded, depthwise[layer], linked, frames)
        input_grads.append(grad_input + grad_hidden)
        batch_point = jnp.stack(point_grads + [grad_res_weight])
        grad_point_acc = grad_point_acc + batch_point
        grad_depth_acc = grad_depth_acc + jnp.stack(depth_grads)
        grad_norm_acc = grad_norm_acc + jnp.stack([jnp.stack(gain_grads), jnp.stack(shift_grads)])
        grad_excite_acc = grad_excite_acc + jnp.stack([grad_down, grad_upward])
    point_shard = lax.psum_scatter(grad_point_acc, ("dp", "tm"), scatter_dimension=1, tiled=True)
    grad_depth, grad_excite = lax.psum((grad_depth_acc, grad_excite_acc * tm_first), ("dp", "tm"))
    pw_moment, pw_square, pw_update = lamb_terms(
        pointwise, pointwise_first, pointwise_second, point_shard
    )
    weight_squares, update_squares = lax.psum(
        (jnp.sum(pointwise * pointwise, axis=(1, 2)), jnp.sum(pw_update * pw_update, axis=(1, 2))),
        ("dp", "tm"),
    )
    pw_wn = jnp.sqrt(weight_squares)
    pw_un = jnp.sqrt(update_squares)
    pw_new = pointwise - RATE * (pw_wn / pw_un)[:, None, None] * pw_update
    dw_moment, dw_square, dw_new, dw_wn, dw_un = local_lamb(
        depthwise, depthwise_first, depthwise_second, grad_depth, (1, 2)
    )
    nm_moment, nm_square, nm_new, nm_wn, nm_un = local_lamb(
        norm_affine, norm_first, norm_second, grad_norm_acc, (2,)
    )
    se_moment, se_square, se_new, se_wn, se_un = local_lamb(
        excite_mats, excite_first, excite_second, grad_excite, (1, 2)
    )
    trust_norms = jnp.stack(
        [
            jnp.concatenate([pw_wn, dw_wn, nm_wn, se_wn]),
            jnp.concatenate([pw_un, dw_un, nm_un, se_un]),
        ]
    )
    block_out = jnp.stack(outputs)[:, None]
    input_grad = jnp.stack(input_grads)[:, None]
    return (
        block_out,
        input_grad,
        pw_moment,
        pw_square,
        pw_new,
        pw_new.astype(jnp.bfloat16),
        dw_moment,
        dw_square,
        dw_new,
        nm_moment,
        nm_square,
        nm_new,
        se_moment,
        se_square,
        se_new,
        trust_norms,
    )


def solution(mesh):
    return jax.shard_map(
        local,
        mesh=mesh,
        in_specs=(
            P(None, "dp", "tm", None),
            P(None, "dp", "tm"),
            P(None, "dp", "tm", None),
            P(None, ("dp", "tm"), None),
            P(None, ("dp", "tm"), None),
            P(None, ("dp", "tm"), None),
            P(),
            P(),
            P(),
            P(),
            P(),
            P(),
            P(),
            P(),
            P(),
        ),
        out_specs=(
            P(None, "dp", "tm", None),
            P(None, "dp", "tm", None),
            P(None, ("dp", "tm"), None),
            P(None, ("dp", "tm"), None),
            P(None, ("dp", "tm"), None),
            P(None, ("dp", "tm"), None),
            P(),
            P(),
            P(),
            P(),
            P(),
            P(),
            P(),
            P(),
            P(),
            P(),
        ),
        check_vma=False,
    )
```

profile of v0, /device:TPU:0, one launch (start us, length us, event | category | flops | bytes accessed | tf_op | source)
XLA Modules:
  0.0 1195.8 jit_solution(7670739850639768876)
XLA Ops:
  9.4 5.6 collective-permute-start.26
  18.0 4.6 collective-permute-start.38
  36.8 4.6 collective-permute-start.2
  65.8 4.8 collective-permute-start.24
  71.9 4.6 collective-permute-start.36
  89.9 42.3 %all-reduce.10 = (f32[512]{0:T(512)S(1)}, f32[]{:T(128)}, f32[512]{0:T(512)S(1)}, f32[512]{0:T(512)S(1)}, f32[]{:T(128)}, /*index=5*/f32[512]{0:T(512)S(1)}, f32...) all-reduce(f32[512]{0:T(512)} %get-tuple-element.275, ...), channel_id=1, replica_groups=mesh['dp'=8,'tm'=4] {'dp','tm'}, use_global_device_ids=true, to_apply=%region_80.0 | all-reduce | flops 4100 | bytes 32800 | tf_op jit(solution)/shard_map/psum | solution.py:150
  156.6 5.1 collective-permute-start.16
  170.6 40.9 %all-reduce.9 = (f32[512]{0:T(512)S(1)}, f32[512]{0:T(512)S(1)}, f32[512]{0:T(512)S(1)}, f32[512]{0:T(512)S(1)}, f32[512]{0:T(512)S(1)}, /*index=5*/f32[512]{0:T(512)S(1)}, f32[512]{0:T(512)S(1)}, f32[512]{0:T(512)S(1)}) all-reduce(f32[512]{0:T(512)S(1)} %get-tuple-element.273, ...), channel_id=1, replica_groups=mesh['dp'=8,'tm'=4] {'dp','tm'}, use_global_device_ids=true, to_apply=%region_84.0 | all-reduce | flops 4096 | bytes 32768 | tf_op jit(solution)/shard_map/psum | solution.py:150
  250.5 40.2 %all-reduce.8 = (f32[512]{0:T(512)S(1)}, f32[512]{0:T(512)S(1)}, f32[512]{0:T(512)S(1)}, f32[512]{0:T(512)S(1)}, f32[512]{0:T(512)S(1)}, /*index=5*/f32[512]{0:T(512)S(1)}, f32[512]{0:T(512)S(1)}, f32[512]{0:T(512)S(1)}) all-reduce(f32[512]{0:T(512)S(1)} %get-tuple-element.271, ...), channel_id=1, replica_groups=mesh['dp'=8,'tm'=4] {'dp','tm'}, use_global_device_ids=true, to_apply=%region_88.0 | all-reduce | flops 4096 | bytes 32768 | tf_op jit(solution)/shard_map/psum | solution.py:150
  329.7 40.5 %all-reduce.7 = (f32[512]{0:T(512)S(1)}, f32[512]{0:T(512)S(1)}, f32[512]{0:T(512)S(1)}, f32[512]{0:T(512)S(1)}, f32[512]{0:T(512)S(1)}, /*index=5*/f32[512]{0:T(512)S(1)}, f32[512]{0:T(512)S(1)}, f32[512]{0:T(512)S(1)}) all-reduce(f32[512]{0:T(512)S(1)} %get-tuple-element.269, ...), channel_id=1, replica_groups=mesh['dp'=8,'tm'=4] {'dp','tm'}, use_global_device_ids=true, to_apply=%region_92.0 | all-reduce | flops 4096 | bytes 32768 | tf_op jit(solution)/shard_map/psum | solution.py:150
  395.6 4.8 collective-permute-start.10
  409.6 39.7 %all-reduce.6 = (f32[512]{0:T(512)S(1)}, f32[512]{0:T(512)S(1)}, f32[512]{0:T(512)S(1)}, f32[512]{0:T(512)S(1)}, f32[512]{0:T(512)S(1)}, /*index=5*/f32[512]{0:T(512)S(1)}, f32[512]{0:T(512)S(1)}, f32[512]{0:T(512)S(1)}) all-reduce(f32[512]{0:T(512)S(1)} %get-tuple-element.267, ...), channel_id=1, replica_groups=mesh['dp'=8,'tm'=4] {'dp','tm'}, use_global_device_ids=true, to_apply=%region_96.0 | all-reduce | flops 4096 | bytes 32768 | tf_op jit(solution)/shard_map/psum | solution.py:150
  456.2 19.5 %all-reduce.12 = (f32[4,512]{1,0:T(4,128)S(1)}, f32[4]{0:T(128)}, f32[4,512]{1,0:T(4,128)S(1)}, f32[4]{0:T(128)}, f32[4,512]{1,0:T(4,128)S(1)}, /*index=5*/f32[4]{0:T(128)}, f32[4,512]{1,0:T(4,128)S(1)}, f32[4]{0:T(128)}) all-reduce(f32[4,512]{1,0:T(4,128)S(1)} %fusion.523, ...), channel_id=1, replica_groups=mesh['dp'=8,'tm'=4] {'tm'}, use_global_device_ids=true, to_apply=%region_97.0 | all-reduce | flops 8208 | bytes 65664 | tf_op jit(solution)/shard_map/psum | solution.py:162
  493.5 16.9 %all-reduce.11 = (f32[4,512]{1,0:T(4,128)}, f32[4,512]{1,0:T(4,128)}, f32[4,512]{1,0:T(4,128)}, f32[4,512]{1,0:T(4,128)S(1)}) all-reduce(f32[4,512]{1,0:T(4,128)S(1)} %fusion.468, f32[4,512]{1,0:T(4,128)S(1)} %fusion.470, f32[4,512]{1,0:T(4,128)S(1)} %fusion.472, f32[4,512]{1,0:T(4,128)S(1)} %fusion.474), channel_id=1, replica_groups=mesh['dp'=8,'tm'=4] {'tm'}, use_global_device_ids=true, to_apply=%region_163.0 | all-reduce | flops 8192 | bytes 65536 | tf_op jit(solution)/shard_map/psum | solution.py:179
  530.6 4.6 multiply_reduce_fusion.19
  543.7 39.0 %all-reduce.5 = (f32[512]{0:T(512)}, f32[512]{0:T(512)}, f32[512]{0:T(512)}, f32[512]{0:T(512)}, f32[512]{0:T(512)}, /*index=5*/f32[512]{0:T(512)}, f32[512]{0:T(512)}, f32[512]{0:T(512)}) all-reduce(f32[512]{0:T(512)} %get-tuple-element.235, f32[512]{0:T(512)} %get-tuple-element.234, ...), channel_id=1, replica_groups=mesh['dp'=8,'tm'=4] {'dp','tm'}, use_global_device_ids=true, to_apply=%region_167.0 | all-reduce | flops 4096 | bytes 32768 | tf_op jit(solution)/shard_map/psum | solution.py:200
  592.0 5.3 collective-permute-start.68
  599.7 5.1 collective-permute-start.78
  613.9 4.5 collective-permute-start.58
  624.4 4.9 collective-permute-start.48
  637.4 42.1 %all-reduce.4 = (f32[512]{0:T(512)S(1)}, f32[512]{0:T(512)S(1)}, f32[512]{0:T(512)S(1)}, f32[512]{0:T(512)S(1)}, f32[512]{0:T(512)S(1)}, /*index=5*/f32[512]{0:T(512)S(1)}, f32[512]{0:T(512)S(1)}, f32[512]{0:T(512)S(1)}) all-reduce(f32[512]{0:T(512)S(1)} %get-tuple-element.233, ...), channel_id=1, replica_groups=mesh['dp'=8,'tm'=4] {'dp','tm'}, use_global_device_ids=true, to_apply=%region_171.0 | all-reduce | flops 4096 | bytes 32768 | tf_op jit(solution)/shard_map/psum | solution.py:200
  711.3 4.9 collective-permute-start.50
  722.9 38.9 %all-reduce.3 = (f32[512]{0:T(512)S(1)}, f32[512]{0:T(512)S(1)}, f32[512]{0:T(512)S(1)}, f32[512]{0:T(512)S(1)}, f32[512]{0:T(512)S(1)}, /*index=5*/f32[512]{0:T(512)S(1)}, f32[512]{0:T(512)S(1)}, f32[512]{0:T(512)S(1)}) all-reduce(f32[512]{0:T(512)S(1)} %get-tuple-element.231, ...), channel_id=1, replica_groups=mesh['dp'=8,'tm'=4] {'dp','tm'}, use_global_device_ids=true, to_apply=%region_175.0 | all-reduce | flops 4096 | bytes 32768 | tf_op jit(solution)/shard_map/psum | solution.py:200
  794.5 4.7 collective-permute-start.52
  808.7 41.6 %all-reduce.2 = (f32[512]{0:T(512)S(1)}, f32[512]{0:T(512)S(1)}, f32[512]{0:T(512)S(1)}, f32[512]{0:T(512)S(1)}, f32[512]{0:T(512)S(1)}, /*index=5*/f32[512]{0:T(512)S(1)}, f32[512]{0:T(512)S(1)}, f32[512]{0:T(512)S(1)}) all-reduce(f32[512]{0:T(512)S(1)} %get-tuple-element.330, ...), channel_id=1, replica_groups=mesh['dp'=8,'tm'=4] {'dp','tm'}, use_global_device_ids=true, to_apply=%region_179.0 | all-reduce | flops 4096 | bytes 32768 | tf_op jit(solution)/shard_map/psum | solution.py:200
  913.7 38.9 %all-reduce.1 = (f32[512]{0:T(512)S(1)}, f32[512]{0:T(512)S(1)}, f32[512]{0:T(512)S(1)}, f32[512]{0:T(512)S(1)}, f32[512]{0:T(512)S(1)}, /*index=5*/f32[512]{0:T(512)S(1)}, f32[512]{0:T(512)S(1)}, f32[512]{0:T(512)S(1)}) all-reduce(f32[512]{0:T(512)S(1)} %get-tuple-element.227, ...), channel_id=1, replica_groups=mesh['dp'=8,'tm'=4] {'dp','tm'}, use_global_device_ids=true, to_apply=%region_183.0 | all-reduce | flops 4096 | bytes 32768 | tf_op jit(solution)/shard_map/psum | solution.py:200
  969.5 5.1 collective-permute-start.86
  979.2 5.1 collective-permute-start.76
  1012.5 14.0 %add_add_fusion = f32[6,512,512]{2,1,0:T(8,128)} fusion(f32[6,512,512]{2,1,0:T(8,128)} %copy-done.32, f32[6,512,512]{2,1,0:T(8,128)} %copy-done.33, f32[6,512,512]{2,1,0:T(8,128)} %copy-done.34, f32[6,512,512]{2,1,0:T(8,128)} %fusion.12), kind=kLoop, calls=%fused_computation | loop fusion | flops 4718592 | bytes 31457280 | tf_op jit(solution)/shard_map/add | solution.py:220
  1047.0 4.9 collective-permute-start.66
  1070.5 73.7 %reduce-scatter.2.cloned.1.call-done = f32[6,16,512]{2,1,0:T(8,128)} async-done(((f32[6,512,512]{2,1,0:T(8,128)}), f32[6,16,512]{2,1,0:T(8,128)}) %reduce-scatter.2.cloned.1.call-update) | async-done | bytes 196624 | tf_op jit(solution)/shard_map/reduce_scatter | solution.py:224
  1145.5 41.1 %all-reduce = (f32[6]{0:T(128)S(1)}, f32[6]{0:T(128)S(1)}, f32[5,5,512]{2,1,0:T(8,128)S(1)}) all-reduce(f32[6]{0:T(128)S(1)} %get-tuple-element.279, f32[6]{0:T(128)S(1)} %get-tuple-element.278, f32[5,5,512]{2,1,0:T(8,128)S(1)} %add_add_fusion.1), channel_id=1, replica_groups=mesh['dp'=8,'tm'=4] {'dp','tm'}, use_global_device_ids=true, to_apply=%region_188.0 | all-reduce | flops 12812 | bytes 102496 | tf_op jit(solution)/shard_map/psum | solution.py:229
  (1593 shorter events, 520.7 us)
Async XLA Ops:
  7.2 73.5 %all-gather.2.cloned.1.call-start = ((), (), s32[]{:S(2)}) async-start(), calls=%async_computation.1 | async-start | bytes 3244032 | tf_op jit(solution)/shard_map/all_gather | solution.py:126
  8.1 28.7 %collective-permute-start.27 = (s32[2]{0:T(128)S(1)}, s32[2]{0:T(128)S(1)}, u32[]{:S(2)}, u32[]{:S(2)}) collective-permute-start(s32[2]{0:T(128)S(1)} %get-tuple-element.695), channel_id=1, source_target_pairs={{1,0},{2,1},{3,2},{5,4},{6,5},{7,6},{9,8},{10,9},{11,10},{13,12},{... | collective-permute-start | bytes 32 | tf_op jit(solution)/shard_map/ppermute | solution.py:27
  9.4 32.0 %collective-permute-start.26 = (s32[2]{0:T(128)S(1)}, s32[2]{0:T(128)S(1)}, u32[]{:S(2)}, u32[]{:S(2)}) collective-permute-start(s32[2]{0:T(128)S(1)} %get-tuple-element.696), channel_id=1, source_target_pairs={{0,1},{1,2},{2,3},{4,5},{5,6},{6,7},{8,9},{9,10},{10,11},{12,13},{... | collective-permute-start | bytes 32 | tf_op jit(solution)/shard_map/ppermute | solution.py:24
  16.6 1051.7 %all-reduce.15.cloned.1.call-start = ((), (), s32[]{:S(2)}) async-start(), calls=%async_computation.3 | async-start | bytes 524288 | tf_op jit(solution)/shard_map/psum | solution.py:225
  16.7 26.1 %collective-permute-start.39 = (s32[2]{0:T(128)S(1)}, s32[2]{0:T(128)S(1)}, u32[]{:S(2)}, u32[]{:S(2)}) collective-permute-start(s32[2]{0:T(128)S(1)} %get-tuple-element.699), channel_id=1, source_target_pairs={{1,0},{2,1},{3,2},{5,4},{6,5},{7,6},{9,8},{10,9},{11,10},{13,12},{... | collective-permute-start | bytes 32 | tf_op jit(solution)/shard_map/ppermute | solution.py:27
  18.0 29.4 %collective-permute-start.38 = (s32[2]{0:T(128)S(1)}, s32[2]{0:T(128)S(1)}, u32[]{:S(2)}, u32[]{:S(2)}) collective-permute-start(s32[2]{0:T(128)S(1)} %get-tuple-element.700), channel_id=1, source_target_pairs={{0,1},{1,2},{2,3},{4,5},{5,6},{6,7},{8,9},{9,10},{10,11},{12,13},{... | collective-permute-start | bytes 32 | tf_op jit(solution)/shard_map/ppermute | solution.py:24
  22.6 26.1 %collective-permute-start.3 = (s32[2]{0:T(128)S(1)}, s32[2]{0:T(128)S(1)}, u32[]{:S(2)}, u32[]{:S(2)}) collective-permute-start(s32[2]{0:T(128)S(1)} %get-tuple-element.687), channel_id=1, source_target_pairs={{1,0},{2,1},{3,2},{5,4},{6,5},{7,6},{9,8},{10,9},{11,10},{13,12},{... | collective-permute-start | bytes 32 | tf_op jit(solution)/shard_map/ppermute | solution.py:27
  41.4 24.4 %collective-permute-start.1 = (bf16[2,512]{1,0:T(2,128)(2,1)S(1)}, bf16[2,512]{1,0:T(2,128)(2,1)S(1)}, u32[]{:S(2)}, u32[]{:S(2)}) collective-permute-start(bf16[2,512]{1,0:T(2,128)(2,1)S(1)} %get-tuple-element.478), channel_id=1, source_target_pairs={{1,0},{2,1},{3,2},{5,4},{6,5},{7,6},{9,8},{10,9},{11,10},{13,12},{... | collective-permute-start | bytes 6152 | tf_op jit(solution)/shard_map/ppermute | solution.py:27
  42.8 27.8 %collective-permute-start = (bf16[2,512]{1,0:T(2,128)(2,1)S(1)}, bf16[2,512]{1,0:T(2,128)(2,1)S(1)}, u32[]{:S(2)}, u32[]{:S(2)}) collective-permute-start(bf16[2,512]{1,0:T(2,128)(2,1)S(1)} %get-tuple-element.472), channel_id=1, source_target_pairs={{0,1},{1,2},{2,3},{4,5},{5,6},{6,7},{8,9},{9,10},{10,11},{12,13},{... | collective-permute-start | bytes 6152 | tf_op jit(solution)/shard_map/ppermute | solution.py:24
  47.3 24.5 %collective-permute-start.13 = (bf16[2,512]{1,0:T(2,128)(2,1)S(1)}, bf16[2,512]{1,0:T(2,128)(2,1)S(1)}, u32[]{:S(2)}, u32[]{:S(2)}) collective-permute-start(bf16[2,512]{1,0:T(2,128)(2,1)S(1)} %get-tuple-element.476), channel_id=1, source_target_pairs={{1,0},{2,1},{3,2},{5,4},{6,5},{7,6},{9,8},{10,9},{11,10},{13,12},{... | collective-permute-start | bytes 6152 | tf_op jit(solution)/shard_map/ppermute | solution.py:27
  48.7 27.7 %collective-permute-start.12 = (bf16[2,512]{1,0:T(2,128)(2,1)S(1)}, bf16[2,512]{1,0:T(2,128)(2,1)S(1)}, u32[]{:S(2)}, u32[]{:S(2)}) collective-permute-start(bf16[2,512]{1,0:T(2,128)(2,1)S(1)} %get-tuple-element.477), channel_id=1, source_target_pairs={{0,1},{1,2},{2,3},{4,5},{5,6},{6,7},{8,9},{9,10},{10,11},{12,13},{... | collective-permute-start | bytes 6152 | tf_op jit(solution)/shard_map/ppermute | solution.py:24
  590.7 23.2 %collective-permute-start.69 = (bf16[2,512]{1,0:T(2,128)(2,1)}, bf16[2,512]{1,0:T(2,128)(2,1)}, u32[]{:S(2)}, u32[]{:S(2)}) collective-permute-start(bf16[2,512]{1,0:T(2,128)(2,1)} %get-tuple-element.521), channel_id=1, source_target_pairs={{1,0},{2,1},{3,2},{5,4},{6,5},{7,6},{9,8},{10,9},{11,10},{13,12},{... | collective-permute-start | bytes 6152 | tf_op jit(solution)/shard_map/ppermute | solution.py:27
  592.0 26.4 %collective-permute-start.68 = (bf16[2,512]{1,0:T(2,128)(2,1)}, bf16[2,512]{1,0:T(2,128)(2,1)}, u32[]{:S(2)}, u32[]{:S(2)}) collective-permute-start(bf16[2,512]{1,0:T(2,128)(2,1)} %get-tuple-element.520), channel_id=1, source_target_pairs={{0,1},{1,2},{2,3},{4,5},{5,6},{6,7},{8,9},{9,10},{10,11},{12,13},{... | collective-permute-start | bytes 6152 | tf_op jit(solution)/shard_map/ppermute | solution.py:24
  598.4 26.0 %collective-permute-start.79 = (bf16[2,512]{1,0:T(2,128)(2,1)}, bf16[2,512]{1,0:T(2,128)(2,1)}, u32[]{:S(2)}, u32[]{:S(2)}) collective-permute-start(bf16[2,512]{1,0:T(2,128)(2,1)} %get-tuple-element.523), channel_id=1, source_target_pairs={{1,0},{2,1},{3,2},{5,4},{6,5},{7,6},{9,8},{10,9},{11,10},{13,12},{... | collective-permute-start | bytes 6152 | tf_op jit(solution)/shard_map/ppermute | solution.py:27
  599.7 29.6 %collective-permute-start.78 = (bf16[2,512]{1,0:T(2,128)(2,1)}, bf16[2,512]{1,0:T(2,128)(2,1)}, u32[]{:S(2)}, u32[]{:S(2)}) collective-permute-start(bf16[2,512]{1,0:T(2,128)(2,1)} %get-tuple-element.522), channel_id=1, source_target_pairs={{0,1},{1,2},{2,3},{4,5},{5,6},{6,7},{8,9},{9,10},{10,11},{12,13},{... | collective-permute-start | bytes 6152 | tf_op jit(solution)/shard_map/ppermute | solution.py:24
  609.9 22.3 %collective-permute-start.59 = (bf16[2,512]{1,0:T(2,128)(2,1)}, bf16[2,512]{1,0:T(2,128)(2,1)}, u32[]{:S(2)}, u32[]{:S(2)}) collective-permute-start(bf16[2,512]{1,0:T(2,128)(2,1)} %get-tuple-element.519), channel_id=1, source_target_pairs={{1,0},{2,1},{3,2},{5,4},{6,5},{7,6},{9,8},{10,9},{11,10},{13,12},{... | collective-permute-start | bytes 6152 | tf_op jit(solution)/shard_map/ppermute | solution.py:27
  613.8 530.4 %reduce-scatter.2.cloned.1.call-start = ((), (), s32[]{:S(2)}) async-start(), calls=%async_computation.2 | async-start | bytes 6488064 | tf_op jit(solution)/shard_map/reduce_scatter | solution.py:224
  686.9 20.8 %collective-permute-start.70 = (bf16[2,512]{1,0:T(2,128)(2,1)S(1)}, bf16[2,512]{1,0:T(2,128)(2,1)S(1)}, u32[]{:S(2)}, u32[]{:S(2)}) collective-permute-start(bf16[2,512]{1,0:T(2,128)(2,1)S(1)} %get-tuple-element.512), channel_id=1, source_target_pairs={{0,1},{1,2},{2,3},{4,5},{5,6},{6,7},{8,9},{9,10},{10,11},{12,13},{... | collective-permute-start | bytes 6152 | tf_op jit(solution)/shard_map/ppermute | solution.py:24
  693.2 23.1 %collective-permute-start.80 = (bf16[2,512]{1,0:T(2,128)(2,1)S(1)}, bf16[2,512]{1,0:T(2,128)(2,1)S(1)}, u32[]{:S(2)}, u32[]{:S(2)}) collective-permute-start(bf16[2,512]{1,0:T(2,128)(2,1)S(1)} %get-tuple-element.514), channel_id=1, source_target_pairs={{0,1},{1,2},{2,3},{4,5},{5,6},{6,7},{8,9},{9,10},{10,11},{12,13},{... | collective-permute-start | bytes 6152 | tf_op jit(solution)/shard_map/ppermute | solution.py:24
  769.1 20.9 %collective-permute-start.72 = (bf16[2,512]{1,0:T(2,128)(2,1)S(1)}, bf16[2,512]{1,0:T(2,128)(2,1)S(1)}, u32[]{:S(2)}, u32[]{:S(2)}) collective-permute-start(bf16[2,512]{1,0:T(2,128)(2,1)S(1)} %get-tuple-element.504), channel_id=1, source_target_pairs={{0,1},{1,2},{2,3},{4,5},{5,6},{6,7},{8,9},{9,10},{10,11},{12,13},{... | collective-permute-start | bytes 6152 | tf_op jit(solution)/shard_map/ppermute | solution.py:24
  774.1 20.4 %collective-permute-start.83 = (bf16[2,512]{1,0:T(2,128)(2,1)S(1)}, bf16[2,512]{1,0:T(2,128)(2,1)S(1)}, u32[]{:S(2)}, u32[]{:S(2)}) collective-permute-start(bf16[2,512]{1,0:T(2,128)(2,1)S(1)} %get-tuple-element.507), channel_id=1, source_target_pairs={{1,0},{2,1},{3,2},{5,4},{6,5},{7,6},{9,8},{10,9},{11,10},{13,12},{... | collective-permute-start | bytes 6152 | tf_op jit(solution)/shard_map/ppermute | solution.py:27
  775.4 23.9 %collective-permute-start.82 = (bf16[2,512]{1,0:T(2,128)(2,1)S(1)}, bf16[2,512]{1,0:T(2,128)(2,1)S(1)}, u32[]{:S(2)}, u32[]{:S(2)}) collective-permute-start(bf16[2,512]{1,0:T(2,128)(2,1)S(1)} %get-tuple-element.506), channel_id=1, source_target_pairs={{0,1},{1,2},{2,3},{4,5},{5,6},{6,7},{8,9},{9,10},{10,11},{12,13},{... | collective-permute-start | bytes 6152 | tf_op jit(solution)/shard_map/ppermute | solution.py:24
  872.1 21.8 %collective-permute-start.75 = (bf16[2,512]{1,0:T(2,128)(2,1)S(1)}, bf16[2,512]{1,0:T(2,128)(2,1)S(1)}, u32[]{:S(2)}, u32[]{:S(2)}) collective-permute-start(bf16[2,512]{1,0:T(2,128)(2,1)S(1)} %get-tuple-element.497), channel_id=1, source_target_pairs={{1,0},{2,1},{3,2},{5,4},{6,5},{7,6},{9,8},{10,9},{11,10},{13,12},{... | collective-permute-start | bytes 6152 | tf_op jit(solution)/shard_map/ppermute | solution.py:27
  873.4 25.1 %collective-permute-start.74 = (bf16[2,512]{1,0:T(2,128)(2,1)S(1)}, bf16[2,512]{1,0:T(2,128)(2,1)S(1)}, u32[]{:S(2)}, u32[]{:S(2)}) collective-permute-start(bf16[2,512]{1,0:T(2,128)(2,1)S(1)} %get-tuple-element.496), channel_id=1, source_target_pairs={{0,1},{1,2},{2,3},{4,5},{5,6},{6,7},{8,9},{9,10},{10,11},{12,13},{... | collective-permute-start | bytes 6152 | tf_op jit(solution)/shard_map/ppermute | solution.py:24
  877.9 24.3 %collective-permute-start.85 = (bf16[2,512]{1,0:T(2,128)(2,1)S(1)}, bf16[2,512]{1,0:T(2,128)(2,1)S(1)}, u32[]{:S(2)}, u32[]{:S(2)}) collective-permute-start(bf16[2,512]{1,0:T(2,128)(2,1)S(1)} %get-tuple-element.499), channel_id=1, source_target_pairs={{1,0},{2,1},{3,2},{5,4},{6,5},{7,6},{9,8},{10,9},{11,10},{13,12},{... | collective-permute-start | bytes 6152 | tf_op jit(solution)/shard_map/ppermute | solution.py:27
  879.2 27.6 %collective-permute-start.84 = (bf16[2,512]{1,0:T(2,128)(2,1)S(1)}, bf16[2,512]{1,0:T(2,128)(2,1)S(1)}, u32[]{:S(2)}, u32[]{:S(2)}) collective-permute-start(bf16[2,512]{1,0:T(2,128)(2,1)S(1)} %get-tuple-element.498), channel_id=1, source_target_pairs={{0,1},{1,2},{2,3},{4,5},{5,6},{6,7},{8,9},{9,10},{10,11},{12,13},{... | collective-permute-start | bytes 6152 | tf_op jit(solution)/shard_map/ppermute | solution.py:24
  883.8 25.3 %collective-permute-start.65 = (bf16[2,512]{1,0:T(2,128)(2,1)}, bf16[2,512]{1,0:T(2,128)(2,1)S(1)}, u32[]{:S(2)}, u32[]{:S(2)}) collective-permute-start(bf16[2,512]{1,0:T(2,128)(2,1)} %get-tuple-element.495), channel_id=1, source_target_pairs={{1,0},{2,1},{3,2},{5,4},{6,5},{7,6},{9,8},{10,9},{11,10},{13,12},{... | collective-permute-start | bytes 6152 | tf_op jit(solution)/shard_map/ppermute | solution.py:27
  968.2 78.8 %collective-permute-start.87 = (bf16[2,512]{1,0:T(2,128)(2,1)}, bf16[2,512]{1,0:T(2,128)(2,1)}, u32[]{:S(2)}, u32[]{:S(2)}) collective-permute-start(bf16[2,512]{1,0:T(2,128)(2,1)} %get-tuple-element.491), channel_id=1, source_target_pairs={{1,0},{2,1},{3,2},{5,4},{6,5},{7,6},{9,8},{10,9},{11,10},{13,12},{... | collective-permute-start | bytes 6152 | tf_op jit(solution)/shard_map/ppermute | solution.py:27
  969.5 82.4 %collective-permute-start.86 = (bf16[2,512]{1,0:T(2,128)(2,1)}, bf16[2,512]{1,0:T(2,128)(2,1)}, u32[]{:S(2)}, u32[]{:S(2)}) collective-permute-start(bf16[2,512]{1,0:T(2,128)(2,1)} %get-tuple-element.490), channel_id=1, source_target_pairs={{0,1},{1,2},{2,3},{4,5},{5,6},{6,7},{8,9},{9,10},{10,11},{12,13},{... | collective-permute-start | bytes 6152 | tf_op jit(solution)/shard_map/ppermute | solution.py:24
  977.7 76.6 %collective-permute-start.77 = (bf16[2,512]{1,0:T(2,128)(2,1)}, bf16[2,512]{1,0:T(2,128)(2,1)}, u32[]{:S(2)}, u32[]{:S(2)}) collective-permute-start(bf16[2,512]{1,0:T(2,128)(2,1)} %get-tuple-element.489), channel_id=1, source_target_pairs={{1,0},{2,1},{3,2},{5,4},{6,5},{7,6},{9,8},{10,9},{11,10},{13,12},{... | collective-permute-start | bytes 6152 | tf_op jit(solution)/shard_map/ppermute | solution.py:27
  979.2 79.7 %collective-permute-start.76 = (bf16[2,512]{1,0:T(2,128)(2,1)}, bf16[2,512]{1,0:T(2,128)(2,1)}, u32[]{:S(2)}, u32[]{:S(2)}) collective-permute-start(bf16[2,512]{1,0:T(2,128)(2,1)} %get-tuple-element.488), channel_id=1, source_target_pairs={{0,1},{1,2},{2,3},{4,5},{5,6},{6,7},{8,9},{9,10},{10,11},{12,13},{... | collective-permute-start | bytes 6152 | tf_op jit(solution)/shard_map/ppermute | solution.py:24
  990.2 69.5 %collective-permute-start.67 = (bf16[2,512]{1,0:T(2,128)(2,1)}, bf16[2,512]{1,0:T(2,128)(2,1)}, u32[]{:S(2)}, u32[]{:S(2)}) collective-permute-start(bf16[2,512]{1,0:T(2,128)(2,1)} %get-tuple-element.487), channel_id=1, source_target_pairs={{1,0},{2,1},{3,2},{5,4},{6,5},{7,6},{9,8},{10,9},{11,10},{13,12},{... | collective-permute-start | bytes 6152 | tf_op jit(solution)/shard_map/ppermute | solution.py:27
  (577 other events, 9472.2 us)
Sparse Core Ops, SparseCore 0:
  16.7 59.8 all-gather.1
  614.0 128.8 all-reduce.14
  1026.6 117.5 reduce-scatter.1
where the time goes:
time: 1210 us; the launch traced here: 1200 us
  blocking collectives  481 us (40%)
  starting transfers between devices  263 us (22%)
  other arithmetic  169 us (14%)
  matrix products  116 us (10%)
  waiting for transfers between devices  80.3 us (7%)
  local copies, waits for them, and re-layouts  63 us (5%)
  between operations  22.8 us (2%)
    ppermute x44, starting transfers between devices, with_halo(): lax.ppermute(lax.slice_in_dim(block, block.shape[dim] - width, None, axis...  205 us
    psum x5, blocking collectives, local(): lax.psum((first_sum, square_sum, jnp.sum(live_mask)), ('dp', 'tm'))  204 us
    psum x5, blocking collectives, local(): sum_grad, sum_cross = lax.psum((sum_grad, sum_cross), ('dp', 'tm'))  200 us
    reduce_scatter x1, waiting for transfers between devices, local(): lax.psum_scatter(grad_point_acc, ('dp', 'tm'), scatter_dimension=1, tiled...  73.7 us
    ppermute x44, starting transfers between devices, with_halo(): lax.ppermute(lax.slice_in_dim(block, 0, width, axis=dim), axis, backward)  57.6 us
    psum x1, blocking collectives, local(): lax.psum((jnp.sum(pointwise * pointwise, axis=(1, 2)), jnp.sum(pw_update...  41.1 us
    unnamed x1055, local copies, waits for them, and re-layouts  32.6 us
    dot_general x20, matrix products, local(): jnp.dot(mixed_low, forward_weights[layer], preferred_element_type=jnp.flo...  29.4 us
  transfers between devices with their start and end apart: 91, of which 4 were waited for; matrix products, arithmetic and copies ran while one was open for 17% of the time, Pallas kernels for 0%

commit v1 on v0

v1 whole, which is shorter than its diff:
```python
import functools

import jax
import jax.numpy as jnp
from jax import lax
from jax.experimental import pallas as pl
from jax.experimental.pallas import tpu as pltpu
from jax.sharding import PartitionSpec as P

NSEG = 4
STEP = 5


BN_EPS = 1e-05
BETA_ONE = 0.5
BETA_TWO = 0.5
LAMB_EPS = 1e-06
DECAY = 0.01
RATE = 1.0
REACH = 2
LANES = 128
ROWS8 = 8
STRIP = 16
WIDE = 4
BLOCK = 256
EDGE = 16
SEGROWS = 16
SCOPED = 56 * 1024 * 1024
F32 = jnp.float32
LOW = jnp.bfloat16
SIDES = (0, 1, 3, 4)


def col(chunk):
    return slice(chunk * LANES, (chunk + 1) * LANES)


def block_rows(block):
    return pl.ds(pl.multiple_of(block * BLOCK, BLOCK), BLOCK)


def strip_rows(index, margin=0):
    return pl.ds(pl.multiple_of(index * STRIP, STRIP), STRIP + 2 * margin)


def middle_rows(index):
    return pl.ds(pl.multiple_of(index * STRIP + EDGE, STRIP), STRIP)


def low_dot(left, right, dims=((1,), (0,))):
    return lax.dot_general(left, right, (dims, ((), ())), preferred_element_type=F32)


def rounded(value):
    return value.astype(LOW).astype(F32)


def tiles(value):
    return value.reshape(-1, ROWS8, value.shape[-1])


def flat(value):
    return value.reshape(-1, value.shape[-1])


def fold(value):
    return jnp.sum(tiles(value), axis=0)


def eight(value):
    return jnp.broadcast_to(value, (ROWS8, value.shape[-1]))


def two_parts(value):
    high = value.astype(LOW)
    return high, (value - high.astype(F32)).astype(LOW)


def three_parts(value):
    high = value.astype(LOW)
    value = value - high.astype(F32)
    middle = value.astype(LOW)
    return jnp.concatenate([high, middle, (value - middle.astype(F32)).astype(LOW)], axis=0)


def summed(ref):
    total = ref[0]
    for index in range(1, ref.shape[0]):
        total = total + ref[index]
    return total


def strips_of(block, strip, carry=0):
    count = BLOCK // STRIP
    return lax.fori_loop(
        0, count, lambda index, value: strip(block * count + index, value), carry, unroll=4
    )


def unrolled_strips_of(block, strip, carry=0):
    count = BLOCK // STRIP
    for index in range(count):
        carry = strip(block * count + index, carry)
    return carry


def wide_strips_of(block, wide_strip):
    count = BLOCK // (STRIP * WIDE)
    lax.fori_loop(0, count, lambda index, carry: wide_strip(block * count + index, carry), 0)


def over_blocks(length, body, carry=0):
    return lax.fori_loop(0, length // BLOCK, body, carry)


def wrap_edges(buffer, chunks, length):
    for chunk in range(chunks):
        for tile in range(2):
            low, high = tile * ROWS8, (tile + 1) * ROWS8
            ends = buffer[chunk, length + low : length + high, :]
            buffer[chunk, low:high, :] = pltpu.roll(ends, 1, 0)
            starts = buffer[chunk, EDGE + low : EDGE + high, :]
            buffer[chunk, EDGE + length + low : EDGE + length + high, :] = pltpu.roll(
                starts, ROWS8 - 1, 0
            )


def into_order(sources, starts, target, chunks, length, edge):
    run = length // ROWS8

    def some(index, carry):
        for source, start in zip(sources, starts, strict=True):
            for part in range(source.shape[0] // run):
                for chunk in range(chunks):
                    rows = pl.ds(pl.multiple_of(part * run + index * 16, 16), 16)
                    value = source[rows, col(chunk)].astype(F32)
                    first = index * 128 + (start + (edge + part))
                    target[chunk, pl.ds(first, 16, stride=ROWS8), :] = value
        return carry

    lax.fori_loop(0, run // 16, some, 0)


def out_of_order(source, target, chunks, length, edge):
    run = length // ROWS8

    def some(index, carry):
        for sublane in range(ROWS8):
            for chunk in range(chunks):
                value = source[chunk, pl.ds(index * 128 + (edge + sublane), 16, stride=ROWS8), :]
                rows = pl.ds(pl.multiple_of(sublane * run + index * 16, 16), 16)
                target[rows, col(chunk)] = value.astype(LOW)
        return carry

    lax.fori_loop(0, run // 16, some, 0)


def send_pieces(me, source, targets, sems):
    count = len(targets)
    size = source.shape[0] // count
    copies = []
    for place in range(count):
        rows = pl.ds(place * size, size)
        step = lax.rem(place - me + count, count) if count > 1 else 0
        for k, target in enumerate(targets):
            copy = pltpu.make_async_copy(source.at[rows], target, sems.at[place])
            if count == 1:
                copy.start()
            else:
                pl.when(step == k)(copy.start)
        copies.append(copy)
    return copies


def write_copies(ref, tops, bottoms):
    for index in range(ref.shape[0]):
        for row, value in enumerate(tops + bottoms):
            ref[index, row : row + 1, :] = value


def norm_terms(stats, inv_total, norm, layer, chunks, par):
    halves = []
    for chunk in range(chunks):
        mean = stats[chunk : chunk + 1] * inv_total
        second = stats[chunks + chunk : chunks + chunk + 1] * inv_total
        inv_std = lax.rsqrt(second - mean * mean + BN_EPS)
        gain = 0.5 * norm[0, layer : layer + 1, col(chunk)] * inv_std
        shift = 0.5 * norm[1, layer : layer + 1, col(chunk)] - mean * gain
        par[0:1, col(chunk)] = mean
        par[1:2, col(chunk)] = inv_std
        par[2:3, col(chunk)] = gain
        par[3:4, col(chunk)] = shift
        halves.append((eight(gain), eight(shift)))
    return halves


def of_stack(matrix_ref, slot):
    return matrix_ref if slot is None else matrix_ref.at[slot]


class Blocks:
    def __init__(self, source, target, sems):
        self.source, self.target, self.sems = source, target, sems
        self.count = source.shape[0] // BLOCK

    def copy(self, block):
        rows = block_rows(block)
        return pltpu.make_async_copy(self.source.at[rows], self.target.at[rows], self.sems.at[block])

    def start(self, block):
        self.copy(block).start()

    def wait(self, block):
        self.copy(block).wait()

    def start_all(self):
        for block in range(self.count):
            self.start(block)
        return self

    def wait_all(self):
        for block in range(self.count):
            self.wait(block)


def bring(sources, targets, sems):
    copies = [
        pltpu.make_async_copy(source, target, sems.at[index])
        for index, (source, target) in enumerate(zip(sources, targets, strict=True))
    ]
    for copy in copies:
        copy.start()
    return copies


def same_utterance(codes, index):
    code = tiles(codes[strip_rows(index, EDGE), :])
    return [code[k : k + 2] == code[2:4] for k in SIDES]


def forward_rest(
    length, channels, layer, codes, depth, taps, buffer, mixed, matrix, point, outs, copies, own
):
    chunks = channels // LANES
    wrap_edges(buffer, chunks, length)
    for k in range(5):
        taps[k] = eight(depth[layer, k : k + 1, :])

    def strip(index, carry):
        same = same_utterance(codes, index)
        for chunk in range(chunks):
            value = tiles(buffer[chunk, strip_rows(index, EDGE), :])
            total = taps[REACH, :, col(chunk)] * value[2:4]
            for slot, k in enumerate(SIDES):
                beside = jnp.where(same[slot], value[k : k + 2], 0.0)
                total = total + taps[k, :, col(chunk)] * beside
            mixed[strip_rows(index), col(chunk)] = flat(total).astype(LOW)
        return carry

    def multiply(block, carry):
        rows = block_rows(block)
        product = low_dot(mixed[rows, :], matrix[...])
        point[rows, :] = product
        if own is not None:
            product = product * own[rows, 0:1]
        return carry[0] + fold(product), carry[1] + fold(product * product)

    def block_step(block, carry):
        carry = multiply(block - 1, carry)
        unrolled_strips_of(block, strip)
        outs[1].start(block - 1)
        outs[0].start(block)
        return carry

    zero = jnp.zeros((ROWS8, channels), F32)
    blocks = length // BLOCK
    strips_of(0, strip)
    outs[0].start(0)
    carry = lax.fori_loop(1, blocks, block_step, (zero, zero))
    first, second = multiply(blocks - 1, carry)
    outs[1].start(blocks - 1)
    first = jnp.sum(first, axis=0, keepdims=True)
    second = jnp.sum(second, axis=0, keepdims=True)
    write_copies(
        copies,
        [first[:, col(chunk)] for chunk in range(chunks)],
        [second[:, col(chunk)] for chunk in range(chunks)],
    )


def send_whole(pairs, sems):
    copies = bring([pair[0] for pair in pairs], [pair[1] for pair in pairs], sems)
    for copy in copies:
        copy.wait()


def piece_starts(me_ref, count):
    if count == 1:
        return [0]
    me = me_ref[0]
    return [lax.rem(me - k + count, count) * (ROWS8 // count) for k in range(count)]


def first_kernel(halo, count, me_ref, *rest):
    x_refs, rest = rest[:count], rest[count:]
    codes_ref, matrix_ref, depth_ref = rest[:3]
    rest = rest[3:]
    own_ref = rest[0] if halo else None
    rest = rest[1:] if halo else rest
    mixed_ref, point_ref, order_ref, copies_ref = rest[:4]
    x, codes, order, depth, copies, taps, matrix, mixed, point, buffer = rest[4:14]
    in_sems, out_sems, whole_sems, last_sems = rest[14:18]
    length, channels = order.shape
    chunks = channels // LANES
    xs = [x.at[pl.ds(k * (length // count), length // count)] for k in range(count)]
    x_in = bring(x_refs, xs, in_sems)
    own = rest[18] if halo else None
    brought = bring(
        [codes_ref, depth_ref, matrix_ref] + ([own_ref] if halo else []),
        [codes, depth, matrix] + ([own] if halo else []),
        whole_sems,
    )
    brought[0].wait()
    for copy in x_in:
        copy.wait()
    into_order(xs, piece_starts(me_ref, count), buffer, chunks, length, EDGE)
    outs = [Blocks(mixed, mixed_ref, out_sems.at[0]), Blocks(point, point_ref, out_sems.at[1])]
    order_out = Blocks(order, order_ref, out_sems.at[2])

    def fill(block, carry):
        def strip(index, carry):
            live = codes[middle_rows(index), :] >= 0.0
            for chunk in range(chunks):
                value = jnp.where(live, buffer[chunk, middle_rows(index), :], 0.0)
                buffer[chunk, middle_rows(index), :] = value
                order[strip_rows(index), col(chunk)] = value.astype(LOW)
            live = live.astype(F32)
            if own is not None:
                live = live * own[strip_rows(index), :]
            return carry + fold(live)

        carry = unrolled_strips_of(block, strip, carry)
        order_out.start(block)
        return carry

    for copy in brought[1:]:
        copy.wait()
    total = over_blocks(length, fill, jnp.zeros((ROWS8, LANES), F32))
    total = eight(jnp.sum(total, axis=0, keepdims=True))
    forward_rest(
        length,
        channels,
        0,
        codes,
        depth,
        taps,
        buffer,
        mixed,
        matrix,
        point,
        outs,
        copies.at[:, 0:ROWS8, :],
        own,
    )
    for index in range(copies.shape[0]):
        copies[index, ROWS8 : 2 * ROWS8, :] = total
    send_whole([(copies, copies_ref)], last_sems)
    for out in outs + [order_out]:
        out.wait_all()


def next_kernel(
    halo,
    layer,
    slot,
    codes_ref,
    before_ref,
    matrix_ref,
    sums_ref,
    norm_ref,
    depth_ref,
    *rest,
):
    if layer > 0:
        inverse_ref, rest = rest[0], rest[1:]
    own_ref = rest[0] if halo else None
    rest = rest[1:] if halo else rest
    mixed_ref, point_ref, copies_ref, par_ref = rest[:4]
    rest = rest[4:]
    if layer == 0:
        inverse_out_ref = rest[0]
        rest = rest[1:]
    codes, before, sums, inverse, norm, par, depth, copies = rest[:8]
    taps, matrix, mixed, point, buffer = rest[8:13]
    in_sems, out_sems, whole_sems, last_sems = rest[13:17]
    own = rest[17] if halo else None
    length, channels = before_ref.shape
    chunks = channels // LANES
    brought = bring(
        [codes_ref, sums_ref, norm_ref] + ([inverse_ref] if layer > 0 else []),
        [codes, sums, norm] + ([inverse] if layer > 0 else []),
        whole_sems.at[0],
    )
    before_in = Blocks(before_ref, before, in_sems).start_all()
    later = bring(
        [depth_ref, of_stack(matrix_ref, slot)] + ([own_ref] if halo else []),
        [depth, matrix] + ([own] if halo else []),
        whole_sems.at[1],
    )
    for copy in brought[1:]:
        copy.wait()
    stats = summed(sums)
    if layer == 0:
        inverse[...] = eight(1.0 / stats[ROWS8 : ROWS8 + 1])
    halves = norm_terms(stats, inverse[0:1, :], norm, layer, chunks, par)
    brought[0].wait()

    def fill(block, carry):
        def strip(index, carry):
            live = codes[middle_rows(index), :] >= 0.0
            for chunk in range(chunks):
                gain, shift = halves[chunk]
                half = tiles(before[strip_rows(index), col(chunk)]) * gain + shift
                value = flat(half * jnp.tanh(half) + half)
                buffer[chunk, middle_rows(index), :] = rounded(jnp.where(live, value, 0.0))
            return carry

        before_in.wait(block)
        unrolled_strips_of(block, strip)
        return carry

    over_blocks(length, fill)
    for copy in later:
        copy.wait()
    outs = [Blocks(mixed, mixed_ref, out_sems.at[0]), Blocks(point, point_ref, out_sems.at[1])]
    forward_rest(
        length,
        channels,
        layer + 1,
        codes,
        depth,
        taps,
        buffer,
        mixed,
        matrix,
        point,
        outs,
        copies,
        own,
    )
    pairs = [(copies, copies_ref), (par, par_ref)]
    if layer == 0:
        pairs.append((inverse, inverse_out_ref))
    send_whole(pairs, last_sems)
    for out in outs:
        out.wait_all()


def squeeze_forward(segment, counts, excite_low):
    pooled_low = (segment / counts).astype(LOW)
    squeeze = low_dot(pooled_low, excite_low[0], ((1,), (1,)))
    half = 0.5 * squeeze
    turned = jnp.tanh(half)
    act = (half * turned + half).astype(LOW)
    gating = 0.5 * jnp.tanh(0.5 * low_dot(act, excite_low[1])) + 0.5
    slope = 0.5 * (1.0 + turned) * (1.0 + half * (1.0 - turned))
    return pooled_low, slope, act, gating


def by_segment(code, rows):
    value = rows[NSEG - 1]
    for index in reversed(range(NSEG - 1)):
        value = jnp.where(code == float(index), rows[index], value)
    return value


def excite_kernel(layer, count, slot, me_ref, *rest):
    cot_refs, rest = rest[:count], rest[count:]
    codes_ref, point_ref, x_ref, matrix_ref, sums_ref, inverse_ref, norm_ref = rest[:7]
    excite_ref = rest[7]
    rest = rest[8:]
    out_refs, rest = rest[:count], rest[count:]
    res_ref, affine_ref, copies_ref, excite_grad_ref, par_ref = rest[:5]
    codes, point, x, cot, matrix, sums, inverse, norm, excite = rest[5:14]
    hidden, residual, total, cot_order, out, res, copies, excite_grad, par = rest[14:23]
    held, sums_of, in_sems, out_sems, whole_sems, last_sems = rest[23:]
    length, channels = point_ref.shape
    chunks = channels // LANES
    first_ones = bring(
        [sums_ref, inverse_ref, norm_ref, codes_ref], [sums, inverse, norm, codes], whole_sems.at[0]
    )
    later = bring([of_stack(matrix_ref, slot), excite_ref], [matrix, excite], whole_sems.at[1])
    point_in = Blocks(point_ref, point, in_sems.at[0])
    x_in = Blocks(x_ref, x, in_sems.at[1])
    for block in range(point_in.count):
        point_in.start(block)
        x_in.start(block)
    cots = [cot.at[pl.ds(k * (length // count), length // count)] for k in range(count)]
    cot_in = bring(cot_refs, cots, in_sems.at[2])
    res_sender = Blocks(res, res_ref, out_sems.at[1])
    affine_sender = Blocks(residual, affine_ref, out_sems.at[2])
    for copy in first_ones[:-1]:
        copy.wait()
    halves = norm_terms(summed(sums), inverse[0:1, :], norm, layer, chunks, par)
    first_ones[-1].wait()
    later[0].wait()
    tile = jnp.zeros((ROWS8, LANES), F32)

    def pool(block, carry):
        def strip(index, carry):
            code = tiles(codes[middle_rows(index), :])
            rows = strip_rows(index)
            new = []
            for chunk in range(chunks):
                gain, shift = halves[chunk]
                half = tiles(point[rows, col(chunk)]) * gain + shift
                value = jnp.where(code >= 0.0, half * jnp.tanh(half) + half, 0.0)
                hidden[rows, col(chunk)] = flat(value)
                for segment in range(NSEG):
                    part = jnp.where(code == float(segment), value, 0.0)
                    new.append(carry[len(new)] + jnp.sum(part, axis=0))
            for segment in range(NSEG):
                part = jnp.where(code == float(segment), 1.0, 0.0)
                new.append(carry[len(new)] + jnp.sum(part, axis=0))
            return tuple(new)

        point_in.wait(block)
        x_in.wait(block)
        rows = block_rows(block)
        residual[rows, :] = low_dot(x[rows, :], matrix[...])
        return unrolled_strips_of(block, strip, carry)

    def hold(carry):
        held[...] = jnp.zeros(held.shape, F32)
        for chunk in range(chunks):
            for index in range(NSEG):
                value = jnp.sum(carry[chunk * NSEG + index], axis=0, keepdims=True)
                held[index : index + 1, col(chunk)] = value
        return held[...]

    pooled = over_blocks(length, pool, (tile,) * ((chunks + 1) * NSEG))
    counts = [jnp.sum(value, axis=0, keepdims=True) for value in pooled[chunks * NSEG :]]
    counts = counts + [jnp.ones((SEGROWS - NSEG, LANES), F32)]
    counts = jnp.concatenate(counts, axis=0)[:, 0:1]
    segment = hold(pooled)
    later[1].wait()
    pooled_low, slope_small, act, gating = squeeze_forward(segment, counts, excite)

    def rows_of(value):
        held[...] = value
        return [
            [eight(held[index : index + 1, col(chunk)]) for index in range(NSEG)]
            for chunk in range(chunks)
        ]

    gates = rows_of(gating)
    for copy in cot_in:
        copy.wait()
    into_order(cots, piece_starts(me_ref, count), cot_order, chunks, length, 0)

    def finish(block, carry):
        def wide_strip(index, carry):
            for chunk in range(chunks):
                found = [None] * NSEG
                for part in range(WIDE):
                    place = index * WIDE + part
                    rows = strip_rows(place)
                    code = tiles(codes[middle_rows(place), :])
                    live = code >= 0.0
                    kept = tiles(hidden[rows, col(chunk)])
                    half = kept * by_segment(code, gates[chunk]) + tiles(residual[rows, col(chunk)])
                    half = 0.5 * half
                    turned = jnp.tanh(half)
                    one = 1.0 + turned
                    value = half * one
                    slope = 0.5 * (one + value * (1.0 - turned))
                    grad = jnp.where(live, tiles(cot_order[chunk, rows, :]) * slope, 0.0)
                    cot_order[chunk, rows, :] = flat(jnp.where(live, value, 0.0))
                    total[rows, col(chunk)] = flat(grad)
                    res[rows, col(chunk)] = flat(grad).astype(LOW)
                    value = grad * kept
                    for k in range(NSEG):
                        new = jnp.sum(jnp.where(code == float(k), value, 0.0), axis=0)
                        found[k] = new if found[k] is None else found[k] + new
                for k in range(NSEG):
                    sums_of[k, :, col(chunk)] += found[k]
            return carry

        wide_strips_of(block, wide_strip)
        res_sender.start(block)
        return carry

    sums_of[...] = jnp.zeros(sums_of.shape, F32)
    over_blocks(length, finish)
    grad_gating = hold(
        [sums_of[k, :, col(chunk)] for chunk in range(chunks) for k in range(NSEG)]
    )
    out_of_order(cot_order, out, chunks, length, 0)
    out_copies = send_pieces(me_ref[0] if count > 1 else 0, out, out_refs, out_sems.at[0])
    grad_low = (grad_gating * gating * (1.0 - gating)).astype(LOW)
    squeeze_low = (low_dot(grad_low, excite[1], ((1,), (1,))) * slope_small).astype(LOW)
    excite_grad[0] = low_dot(squeeze_low, pooled_low, ((0,), (0,)))
    excite_grad[1] = low_dot(act, grad_low, ((0,), (0,)))
    lifts = rows_of(low_dot(squeeze_low, excite[0]) / counts)

    def begin_back(block, carry):

        def wide_strip(index, carry):
            for chunk in range(chunks):
                gain, shift = halves[chunk]
                plain = cross = None
                for part in range(WIDE):
                    place = index * WIDE + part
                    rows = strip_rows(place)
                    code = tiles(codes[middle_rows(place), :])
                    product = tiles(point[rows, col(chunk)])
                    half = product * gain + shift
                    turned = jnp.tanh(half)
                    one = 1.0 + turned
                    slope = 0.5 * (one + half * one * (1.0 - turned))
                    grad = tiles(total[rows, col(chunk)]) * by_segment(code, gates[chunk])
                    lift = jnp.where(code >= 0.0, by_segment(code, lifts[chunk]), 0.0)
                    grad = (grad + lift) * slope
                    residual[rows, col(chunk)] = flat(grad)
                    new = jnp.sum(grad, axis=0)
                    plain = new if plain is None else plain + new
                    new = jnp.sum(grad * product, axis=0)
                    cross = new if cross is None else cross + new
                sums_of[0, :, col(chunk)] += plain
                sums_of[1, :, col(chunk)] += cross
            return carry

        wide_strips_of(block, wide_strip)
        affine_sender.start(block)
        return carry

    sums_of[...] = jnp.zeros(sums_of.shape, F32)
    over_blocks(length, begin_back)
    carries = [[sums_of[i, :, col(chunk)] for i in range(2)] for chunk in range(chunks)]
    gradient_sums(carries, par, copies)
    send_whole(
        [(copies, copies_ref), (excite_grad, excite_grad_ref), (par, par_ref)], last_sems
    )
    for copy in out_copies:
        copy.wait()
    for sender in (res_sender, affine_sender):
        sender.wait_all()


def gradient_sums(carries, par, copies):
    tops, bottoms = [], []
    for chunk, carry in enumerate(carries):
        plain = jnp.sum(carry[0], axis=0, keepdims=True)
        cross = jnp.sum(carry[1], axis=0, keepdims=True)
        mean = par[0:1, col(chunk)]
        tops.append(plain)
        bottoms.append((cross - mean * plain) * par[1:2, col(chunk)])
    write_copies(copies, tops, bottoms)


def back_kernel(halo, layer, share, count, slot, third_slot, me_ref, *rest):
    codes_ref, affine_ref, point_ref, before_ref, matrix_ref = rest[:5]
    rest = rest[5:]
    if layer == 0:
        res_ref, third_ref = rest[:2]
        rest = rest[2:]
    small_refs = rest[:5]
    rest = rest[5:]
    if layer > 0:
        prior_ref = rest[0]
        rest = rest[1:]
    own_ref = rest[0] if halo else None
    rest = rest[1:] if halo else rest
    low_ref, small_ref = rest[:2]
    rest = rest[2:]
    if layer > 0:
        next_ref, copies_ref = rest[:2]
        rest = rest[2:]
    else:
        next_refs, rest = rest[:count], rest[count:]
    codes, affine, point, before, matrix, low, after, buffer, sums, inverse, norm = rest[:11]
    depth, par, small, sums_of, taps = rest[11:16]
    in_sems, out_sems, whole_sems, last_sems = rest[16:20]
    rest = rest[20:]
    own = rest[-1] if halo else None
    length, channels = point_ref.shape
    chunks = channels // LANES
    brought = bring(
        list(small_refs) + [codes_ref], [sums, inverse, norm, depth, par, codes], whole_sems.at[0]
    )
    affine_in = Blocks(affine_ref, affine, in_sems.at[0])
    point_in = Blocks(point_ref, point, in_sems.at[1])
    affine_in.start(0)
    point_in.start(0)
    sources, targets = [of_stack(matrix_ref, slot)], [matrix]
    if layer == 0:
        res, third, lifted = rest[:3]
        sources.append(of_stack(third_ref, third_slot))
        targets.append(third)
    else:
        prior, copies = rest[:2]
        sources.append(prior_ref)
        targets.append(prior)
    if halo:
        sources.append(own_ref)
        targets.append(own)
    later = bring(sources, targets, whole_sems.at[1])
    if layer == 0:
        res_in = Blocks(res_ref, res, in_sems.at[3])
        res_in.start(0)
    for block in range(1, affine_in.count):
        affine_in.start(block)
        point_in.start(block)
        if layer == 0:
            res_in.start(block)
    before_in = Blocks(before_ref, before, in_sems.at[2]).start_all()
    low_sender = Blocks(low, low_ref, out_sems.at[0])
    if layer > 0:
        next_sender = Blocks(after, next_ref, out_sems.at[1])
    for copy in brought[:-1]:
        copy.wait()
    stats = summed(sums)
    inv_total = inverse[0:1, :]
    scale = []
    norm_grads = []
    for chunk in range(chunks):
        plain = stats[chunk : chunk + 1]
        cross = stats[chunks + chunk : chunks + chunk + 1]
        norm_grads.append([cross * share, plain * share])
        mean = par[0:1, col(chunk)]
        inv_std = par[1:2, col(chunk)]
        outer = norm[0, layer : layer + 1, col(chunk)] * inv_std
        slope = outer * inv_std * cross * inv_total
        offset = outer * plain * inv_total - slope * mean
        scale.append((eight(outer), eight(slope), eight(offset)))
    brought[-1].wait()

    def strip(index, carry):
        live = codes[middle_rows(index), :] >= 0.0
        rows = strip_rows(index)
        for chunk in range(chunks):
            outer, slope, offset = scale[chunk]
            value = tiles(affine[rows, col(chunk)]) * outer
            value = value - tiles(point[rows, col(chunk)]) * slope - offset
            low[rows, col(chunk)] = jnp.where(live, flat(value), 0.0).astype(LOW)
        return carry

    def multiply(block):
        rows = block_rows(block)
        grad = rounded(low_dot(low[rows, :], matrix[...], ((1,), (1,))))
        inner = pl.ds(pl.multiple_of(block * BLOCK + EDGE, EDGE), BLOCK)
        for chunk in range(chunks):
            buffer[chunk, inner, :] = grad[:, col(chunk)]
        if layer == 0:
            lift = low_dot(res[rows, :], third[...], ((1,), (1,)))
            for chunk in range(chunks):
                lifted[chunk, rows, :] = lift[:, col(chunk)]

    def block_step(block, carry):
        affine_in.wait(block)
        point_in.wait(block)
        if layer == 0:
            res_in.wait(block - 1)
        multiply(block - 1)
        unrolled_strips_of(block, strip)
        low_sender.start(block)
        return carry

    blocks = length // BLOCK
    affine_in.wait(0)
    point_in.wait(0)
    strips_of(0, strip)
    low_sender.start(0)
    for copy in later:
        copy.wait()
    lax.fori_loop(1, blocks, block_step, 0)
    if layer == 0:
        res_in.wait(blocks - 1)
    multiply(blocks - 1)
    wrap_edges(buffer, chunks, length)
    kinds = 7 if layer > 0 else 5
    sums_of[...] = jnp.zeros(sums_of.shape, F32)
    for k in range(5):
        tap = depth[layer, k : k + 1, :]
        taps[k] = eight(0.5 * tap if layer > 0 else tap)
    if layer > 0:
        taps[5] = eight(prior[2:3, :])
        taps[6] = eight(prior[3:4, :])

    def unmix(block, carry):
        before_in.wait(block)

        def wide_strip(index, carry):
            for chunk in range(chunks):
                kernel = [taps[k, :, col(chunk)] for k in range(5)]
                if layer > 0:
                    gain, shift = taps[5, :, col(chunk)], taps[6, :, col(chunk)]
                found = [None] * kinds
                for part in range(WIDE):
                    place = index * WIDE + part
                    rows = strip_rows(place)
                    value = tiles(buffer[chunk, strip_rows(place, EDGE), :])
                    same = same_utterance(codes, place)
                    terms = [value[k : k + 2] for k in range(5)]
                    for slot, k in enumerate(SIDES):
                        terms[k] = jnp.where(same[slot], terms[k], 0.0)
                    grad = kernel[REACH] * terms[REACH]
                    for k in SIDES:
                        grad = grad + kernel[4 - k] * terms[k]
                    if layer > 0:
                        product = tiles(before[rows, col(chunk)])
                        half = product * gain + shift
                        turned = jnp.tanh(half)
                        one = 1.0 + turned
                        hidden = half * one
                        grad = grad * (one + hidden * (1.0 - turned))
                        hidden = tiles(rounded(flat(hidden)))
                        after[rows, col(chunk)] = flat(grad)
                    else:
                        hidden = tiles(before[rows, col(chunk)].astype(F32))
                        lifted[chunk, rows, :] = flat(grad) + lifted[chunk, rows, :]
                    if own is not None:
                        inside = tiles(own[rows, :])
                        hidden = hidden * inside
                        grad = grad * inside
                    new = [jnp.sum(hidden * terms[4 - k], axis=0) for k in range(5)]
                    if layer > 0:
                        new += [jnp.sum(grad, axis=0), jnp.sum(grad * product, axis=0)]
                    found = [b if a is None else a + b for a, b in zip(found, new, strict=True)]
                for k in range(kinds):
                    sums_of[k, :, col(chunk)] += found[k]
            return carry

        wide_strips_of(block, wide_strip)
        if layer > 0:
            next_sender.start(block)
        return carry

    over_blocks(length, unmix)
    if layer == 0:
        out_of_order(lifted, after, chunks, length, 0)
        me = me_ref[0] if count > 1 else 0
        piece_copies = send_pieces(me, after, next_refs, out_sems.at[1])
    for chunk in range(chunks):
        tile = [jnp.sum(sums_of[k, :, col(chunk)], axis=0, keepdims=True) for k in range(5)]
        tile += norm_grads[chunk] + [jnp.zeros((SEGROWS - 7, LANES), F32)]
        small[:, col(chunk)] = jnp.concatenate(tile, axis=0).astype(LOW)
    pairs = [(small, small_ref)]
    if layer > 0:
        carries = [[sums_of[5 + i, :, col(chunk)] for i in range(2)] for chunk in range(chunks)]
        gradient_sums(carries, prior, copies)
        pairs.append((copies, copies_ref))
    send_whole(pairs, last_sems)
    low_sender.wait_all()
    if layer > 0:
        next_sender.wait_all()
    else:
        for copy in piece_copies:
            copy.wait()


def run(body, me, args, outs, scratch, flops=0):
    there = pl.BlockSpec(memory_space=pl.ANY)
    first = [pl.BlockSpec(memory_space=pltpu.SMEM)] * len(me)
    moved = sum(a.size * a.dtype.itemsize for a in args)
    return pl.pallas_call(
        body,
        out_shape=[jax.ShapeDtypeStruct(shape, dtype) for shape, dtype in outs],
        in_specs=first + [there] * len(args),
        out_specs=[there] * len(outs),
        scratch_shapes=[
            piece if not isinstance(piece, tuple) else pltpu.VMEM(*piece) for piece in scratch
        ],
        compiler_params=pltpu.CompilerParams(vmem_limit_bytes=SCOPED),
        cost_estimate=pl.CostEstimate(flops=flops, bytes_accessed=moved, transcendentals=0),
    )(*me, *args)


def close(value):
    return pltpu.with_memory_space_constraint(value, pltpu.VMEM)


def exchange(blocks, axis):
    return lax.all_to_all(blocks, axis, 0, 0)


def copies_of(block, count):
    return jnp.broadcast_to(block[None], (count,) + block.shape)


def swish_slope(value):
    sigma = jax.nn.sigmoid(value)
    return sigma * (1.0 + value * (1.0 - sigma))


def lamb_terms(weights, first, second, grads):
    first_new = BETA_ONE * first + (1.0 - BETA_ONE) * grads
    second_new = BETA_TWO * second + (1.0 - BETA_TWO) * grads * grads
    first_hat = first_new / (1.0 - BETA_ONE**STEP)
    second_hat = second_new / (1.0 - BETA_TWO**STEP)
    update = first_hat / (jnp.sqrt(second_hat) + LAMB_EPS) + DECAY * weights
    return (first_new, second_new, update)


def finish_kernel(small_rows, *refs):
    gathered, weights, updates = refs[:3]
    depth, norm, excite = refs[3:6], refs[6:9], refs[9:12]
    new_ref, half_ref = refs[12:14]
    depth_out, norm_out, excite_out = refs[14:17], refs[17:20], refs[20:23]
    trust_ref, rows, spread = refs[23:]
    each = small_rows + 1
    matrices = weights.shape[0]
    convs, taps = depth[0].shape[:2]
    rows[...] = gathered[...].astype(F32)

    def row(index):
        place = index // small_rows * each + index % small_rows
        return rows[place : place + 1, :]

    squares = rows[small_rows : small_rows + 1, :]
    for device in range(1, gathered.shape[0] // each):
        place = device * each + small_rows
        squares = squares + rows[place : place + 1, :]
    squares = squares[:, col(0)] + squares[:, col(1)] + squares[:, col(2)]
    norms = [
        (jnp.sqrt(squares[:, m : m + 1]), jnp.sqrt(squares[:, matrices + m : matrices + m + 1]))
        for m in range(matrices)
    ]
    for m, (weight_norm, update_norm) in enumerate(norms):
        new = weights[m] - RATE * (weight_norm / update_norm) * updates[m]
        new_ref[m] = new
        half_ref[m] = new.astype(LOW)

    def total(value):
        return jnp.sum(jnp.sum(value, axis=1, keepdims=True), axis=0, keepdims=True)

    def step(old, grad):
        first, second, update = lamb_terms(*old, grad)
        weight_norm = jnp.sqrt(total(old[0] * old[0]))
        update_norm = jnp.sqrt(total(update * update))
        new = old[0] - RATE * (weight_norm / update_norm) * update
        return (first, second, new), (weight_norm, update_norm)

    sides = [[], []]
    for layer in range(convs):
        base = layer * SEGROWS
        grad = jnp.concatenate([row(base + k) for k in range(taps)], axis=0)
        results, pair = step([ref[layer] for ref in depth], grad)
        for ref, result in zip(depth_out, results, strict=True):
            ref[layer] = result
        norms.append(pair)
        for side in range(2):
            old = [ref[layer, side : side + 1, :] for ref in norm]
            results, pair = step(old, row(base + taps + side))
            for ref, result in zip(norm_out, results, strict=True):
                ref[layer, side : side + 1, :] = result
            sides[side].append(pair)
    norms += sides[0] + sides[1]
    base = convs * SEGROWS
    for index in range(spread.shape[0]):
        spread[index : index + 1, :] = row(base + index)
    size = excite[0].shape[1]
    for side in range(2):
        grad = spread[side * size : (side + 1) * size, :]
        results, pair = step([ref[side] for ref in excite], grad)
        for ref, result in zip(excite_out, results, strict=True):
            ref[side] = result
        norms.append(pair)
    lane = lax.broadcasted_iota(jnp.int32, (1, LANES), 1)
    for side in range(2):
        line = jnp.zeros((1, LANES), F32)
        for index, pair in enumerate(norms):
            line = jnp.where(lane == index, pair[side], line)
        trust_ref[side : side + 1, :] = line[:, : len(norms)]


def local_lamb(weights, first, second, grads, axes):
    first_new, second_new, update = lamb_terms(weights, first, second, grads)
    weight_norm = jnp.sqrt(jnp.sum(weights * weights, axis=axes, keepdims=True))
    update_norm = jnp.sqrt(jnp.sum(update * update, axis=axes, keepdims=True))
    weights_new = weights - RATE * (weight_norm / update_norm) * update
    return (first_new, second_new, weights_new, weight_norm.reshape(-1), update_norm.reshape(-1))


def local(
    inputs,
    utterance_ids,
    cotangent,
    pointwise,
    pointwise_first,
    pointwise_second,
    depthwise,
    depthwise_first,
    depthwise_second,
    norm_affine,
    norm_first,
    norm_second,
    excite_mats,
    excite_first,
    excite_second,
):
    batches, _, frames, channels = inputs.shape
    convs, taps = depthwise.shape[:2]
    matrices, shard_rows = pointwise.shape[:2]
    chunks = channels // LANES
    across_dp = lax.axis_size("dp")
    across_tm = lax.axis_size("tm")
    parts = across_tm // batches
    own = frames * batches
    width = BLOCK // 2 if parts > 1 else 0
    length = own + 2 * width
    groups = None
    partners = None
    if parts > 1:
        groups = [[part * batches + b for b in range(batches)] for part in range(parts)]
        partners = [[part * batches + b for part in range(parts)] for b in range(batches)]

    def over_rows(block):
        return lax.all_to_all(block, "tm", 0, 0, axis_index_groups=groups)

    def to_next(piece, step):
        return lax.ppermute(piece, "tm", [(i, (i + step) % batches) for i in range(batches)])

    def with_permutes(pieces):
        return pieces[:1] + [to_next(pieces[k], k) for k in range(1, batches)]

    def step_pieces(block):
        if parts > 1:
            return [over_rows(block)]
        return with_permutes(
            [
                lax.dynamic_index_in_dim(block, lax.rem(me + step, batches), 0, keepdims=False)
                for step in range(batches)
            ]
        )

    def settle(pieces):
        if parts > 1:
            return pieces[0]
        placed = []
        for source in range(batches):
            distance = lax.rem(me - source + batches, batches)
            piece = pieces[0]
            for step in range(1, batches):
                piece = jnp.where(distance == step, pieces[step], piece)
            placed.append(piece)
        return jnp.stack(placed)

    def over_parts(value):
        if parts == 1:
            return value
        return lax.psum(value, "tm", axis_index_groups=partners)

    def with_neighbours(block):
        if parts == 1:
            return block
        forward = [(i, i + batches) for i in range(across_tm - batches)]
        backward = [(target, source) for source, target in forward]
        before = lax.ppermute(block[-width:], "tm", forward)
        after = lax.ppermute(block[:width], "tm", backward)
        return jnp.concatenate([block, after, before], axis=0)

    def own_sums(copies):
        if parts > 1:
            copies = copies_of(over_parts(copies[0]), across_dp)
        sums = exchange(copies, "dp")
        return close(sums) if parts == 1 else sums

    me = lax.axis_index("tm")
    id_rows = -(-frames // channels)
    ids_low = jnp.pad(utterance_ids[:, 0], ((0, 0), (0, id_rows * channels - frames)))
    ids_low = ids_low.astype(LOW).reshape(batches, id_rows, channels)
    both = copies_of(pointwise[:2].astype(LOW).reshape(2 * shard_rows, channels), across_tm)
    early = exchange(jnp.concatenate([both, jnp.concatenate([ids_low] * parts, axis=0)], axis=1), "tm")
    early, x_held = lax.optimization_barrier((early, inputs))
    if parts == 1:
        first = lax.dynamic_index_in_dim(inputs[:, 0], lax.rem(me + 1, batches), 0, keepdims=False)
        x_pieces = step_pieces(x_held[:, 0])
        x_pieces[1] = to_next(first, 1)
    else:
        x_pieces = [with_neighbours(over_rows(x_held[:, 0]).reshape(own, channels))]
    ids_own = early[:, 2 * shard_rows : 2 * shard_rows + id_rows].reshape(across_tm, -1)[:, :frames]
    if parts > 1:
        ids_own = lax.dynamic_slice_in_dim(ids_own, me // batches * batches, batches, 0)
    ids_own = ids_own.astype(jnp.int32).reshape(own)
    late = lax.all_gather(pointwise[2:].astype(LOW), ("dp", "tm"), axis=1, tiled=True)
    excite_low = excite_mats.astype(LOW)
    ids = with_neighbours(ids_own[:, None] + 1)[:, 0] - 1
    run_length = length // ROWS8
    place = jnp.arange(length, dtype=jnp.int32)
    code = jnp.where(ids >= 0, ids, -2 - place).astype(F32)
    if parts == 1:
        head = (-2 - length - jnp.arange(REACH, dtype=jnp.int32)).astype(F32)
        tail = head - REACH
    else:
        head, tail = code[-REACH:], code[:REACH]
    code = jnp.concatenate([head, code, tail])
    code = jnp.stack(
        [code[s * run_length : (s + 1) * run_length + 2 * REACH] for s in range(ROWS8)], axis=1
    )
    codes = jnp.broadcast_to(code.reshape(-1)[:, None], (length + 2 * EDGE, LANES))

    early = [
        early[:, i * shard_rows : (i + 1) * shard_rows].reshape(-1, channels) for i in range(2)
    ]
    early[0] = lax.all_gather(early[0], "dp", tiled=True)
    early[0], early[1], codes = lax.optimization_barrier((early[0], early[1], codes))
    early[1] = lax.all_gather(early[1], "dp", tiled=True)
    x_pieces[0], early = lax.optimization_barrier((x_pieces[0], early))

    def in_order(values):
        return jnp.swapaxes(values.reshape((ROWS8, run_length) + values.shape[1:]), 0, 1).reshape(
            values.shape
        )

    def in_time(values):
        return jnp.swapaxes(values.reshape((run_length, ROWS8) + values.shape[1:]), 0, 1).reshape(
            values.shape
        )

    ids_order = in_order(ids)
    own_order = in_order(place) < own
    halo = [jnp.broadcast_to(own_order.astype(F32)[:, None], (length, LANES))] if parts > 1 else []
    wide = (length, channels)
    blocks = length // BLOCK
    code_shape = (codes.shape, F32)
    buffer = ((chunks, length + 2 * EDGE, LANES), F32)
    split = ((chunks, length, LANES), F32)
    square = ((channels, channels), LOW)
    copies = ((across_dp, 2 * chunks, LANES), F32)
    par = ((ROWS8, channels), F32)
    product = 2 * length * channels * channels

    def sems(*shape):
        return pltpu.SemaphoreType.DMA(shape)

    here = [me.astype(jnp.int32).reshape(1)]
    norm_shape, depth_shape = (norm_affine.shape, F32), (depthwise.shape, F32)
    tile_shape = ((ROWS8, LANES), F32)
    own_shape = [((length, LANES), F32)] * len(halo)
    mixed, points, pars = [None] * convs, [None] * convs, [None] * convs
    forward_scratch = [((taps, ROWS8, channels), F32), square, (wide, LOW), (wide, F32), buffer]
    first_copies = ((across_dp, 2 * ROWS8, LANES), F32)
    weights = early + [None] * (matrices - 2)
    slots = [None, None] + list(range(matrices - 2))
    mixed[0], points[0], x_order, sums = run(
        functools.partial(first_kernel, bool(halo), len(x_pieces)),
        here,
        [close(piece) if parts == 1 else piece for piece in x_pieces]
        + [codes, weights[0], depthwise]
        + halo,
        [(wide, LOW), (wide, F32), (wide, LOW), first_copies],
        [(wide, LOW), code_shape, (wide, LOW), depth_shape, first_copies]
        + forward_scratch
        + [sems(blocks), sems(3, blocks), sems(4), sems(1)]
        + own_shape,
        product,
    )
    weights[2:] = [late] * (matrices - 2)
    sums = own_sums(sums)
    inverse = []
    for layer in range(convs - 1):
        extra = [tile_shape] if layer == 0 else []
        result = run(
            functools.partial(next_kernel, bool(halo), layer, slots[layer + 1]),
            [],
            [codes, points[layer], weights[layer + 1], sums, norm_affine, depthwise]
            + inverse
            + halo,
            [(wide, LOW), (wide, F32), copies, par] + extra,
            [code_shape, (wide, F32), (sums.shape, F32), tile_shape, norm_shape, par]
            + [depth_shape, copies]
            + forward_scratch
            + [sems(blocks), sems(2, blocks), sems(2, 4), sems(3)]
            + own_shape,
            product,
        )
        mixed[layer + 1], points[layer + 1], sums, pars[layer] = result[:4]
        if layer == 0:
            inverse = [result[4]]
            cot_held, sums = lax.optimization_barrier((cotangent, sums))
            cot_pieces = step_pieces(cot_held[:, 0])
        sums = own_sums(sums)
    last = convs - 1
    if parts == 1:
        excite_shape = (excite_mats.shape, F32)
        piece = ((frames, channels), LOW)
        result = run(
            functools.partial(excite_kernel, last, len(cot_pieces), slots[convs]),
            here,
            [close(piece) for piece in cot_pieces]
            + [codes, points[last], x_order, weights[convs], sums, inverse[0], norm_affine]
            + [excite_low],
            [piece] * batches + [(wide, LOW), (wide, F32), copies, excite_shape, par],
            [code_shape, (wide, F32), (wide, LOW), (wide, LOW), square, copies, tile_shape]
            + [norm_shape, (excite_low.shape, LOW)]
            + [(wide, F32)] * 3
            + [split]
            + [(wide, LOW)] * 2
            + [copies, excite_shape, par, ((SEGROWS, channels), F32)]
            + [((ROWS8, ROWS8, channels), F32)]
            + [sems(3, blocks), sems(3, blocks), sems(2, 4), sems(3)],
            product,
        )
        out_pieces = with_permutes(list(result[:batches]))
        grad_res, affine, sums, excite_grad, pars[last] = result[batches:]
    else:
        stats = jnp.sum(sums, axis=0).reshape(2, channels)
        mean = stats[0] * inverse[0][0, 0]
        inv_std = lax.rsqrt(stats[1] * inverse[0][0, 0] - mean * mean + BN_EPS)
        gain = norm_affine[0, last] * inv_std
        shift = norm_affine[1, last] - mean * gain
        pars[last] = jnp.pad(jnp.stack([mean, inv_std, 0.5 * gain, 0.5 * shift]), ((0, 4), (0, 0)))
        mask = (ids_order >= 0).astype(F32)[:, None]
        own_mask = own_order.astype(F32)[:, None]
        value = points[last] * gain + shift
        hidden = value * jax.nn.sigmoid(value) * mask
        segment_index = jnp.arange(SEGROWS, dtype=jnp.int32)
        onehot = ids_order[None, :] == jnp.where(segment_index < NSEG, segment_index, -9)[:, None]
        onehot = onehot.astype(F32)

        def gather(values):
            values = jnp.dot(onehot, values * own_mask, precision=lax.Precision.HIGHEST)
            return over_parts(values)

        def pick(values):
            return jnp.dot(onehot.T, values, precision=lax.Precision.HIGHEST)

        count = over_parts(jnp.dot(onehot, own_mask, precision=lax.Precision.HIGHEST))
        count = jnp.where(segment_index < NSEG, count[:, 0], 1.0)[:, None]
        pooled_low, slope_small, act, gating = squeeze_forward(gather(hidden), count, excite_low)
        spread = pick(gating)
        total = hidden * spread + low_dot(x_order, weights[convs][slots[convs]])
        block_out = in_time((total * jax.nn.sigmoid(total) * mask).astype(LOW))
        out_pieces = [over_rows(block_out[:own].reshape(batches, frames, channels))]
        cot_low = with_neighbours(cot_pieces[0].reshape(own, channels))
        grad_total = in_order(cot_low).astype(F32) * mask * swish_slope(total)
        grad_res = grad_total.astype(LOW)
        grad_low = (gather(grad_total * hidden) * gating * (1.0 - gating)).astype(LOW)
        squeeze_low = (low_dot(grad_low, excite_low[1], ((1,), (1,))) * slope_small).astype(LOW)
        excite_grad = jnp.stack(
            [
                low_dot(squeeze_low, pooled_low, ((0,), (0,))),
                low_dot(act, grad_low, ((0,), (0,))),
            ]
        )
        affine = grad_total * spread + pick(low_dot(squeeze_low, excite_low[0]) / count)
        affine = affine * swish_slope(value)
        plain = jnp.sum(affine * own_mask, axis=0)
        cross = jnp.sum(affine * own_mask * (points[last] - mean) * inv_std, axis=0)
        sums = copies_of(jnp.stack([plain, cross]).reshape(2 * chunks, LANES), across_dp)

    def weight_grad(left, right):
        if parts > 1:
            left = left * own_order.astype(LOW)[:, None]
        return low_dot(left, right, ((0,), (0,)))

    def to_row(grads):
        grads = grads.astype(LOW)
        return lax.psum_scatter(grads, "dp", scatter_dimension=1, tiled=True)

    share = 1.0 / (across_dp * parts)
    point_grads = [None] * matrices
    point_grads[convs] = weight_grad(x_order, grad_res)
    small_grads = [None] * convs
    small_tile = ((SEGROWS, channels), LOW)
    for layer in reversed(range(convs)):
        sums = own_sums(sums)
        arrived = convs - 2 - layer
        if 0 < arrived < len(out_pieces):
            sums, out_pieces[arrived] = lax.optimization_barrier((sums, out_pieces[arrived]))
        near_args = [sums, inverse[0], norm_affine, depthwise, pars[layer]]
        scratch = [code_shape, (wide, F32), (wide, F32), None, square, (wide, LOW), None, buffer]
        scratch += [copies, tile_shape, norm_shape, depth_shape, par, small_tile]
        scratch += [((ROWS8, ROWS8, channels), F32)] * 2
        args = [codes, affine, points[layer]]
        if layer > 0:
            args += [points[layer - 1], weights[layer]] + near_args + [pars[layer - 1]]
            scratch[3], scratch[6] = (wide, F32), (wide, F32)
            scratch += [sems(3, blocks), sems(2, blocks), sems(2, 6), sems(2), par, copies]
            outs = [(wide, LOW), small_tile, (wide, F32), copies]
        else:
            args += [x_order, weights[layer], grad_res, weights[convs]] + near_args
            scratch[3], scratch[6] = (wide, LOW), (wide, LOW)
            scratch += [sems(4, blocks), sems(3, blocks), sems(2, 6), sems(2)]
            scratch += [(wide, LOW), square, split]
            outs = [(wide, LOW), small_tile]
            whole = ((frames, channels), LOW)
            outs += [(wide, LOW)] if parts > 1 else [whole] * batches
        result = run(
            functools.partial(
                back_kernel,
                bool(halo),
                layer,
                share,
                batches if parts == 1 else 1,
                slots[layer],
                slots[convs],
            ),
            here,
            args + halo,
            outs,
            scratch + own_shape,
            2 * product,
        )
        grad_low, small_grads[layer] = result[:2]
        if layer > 0:
            affine, sums = result[2:]
        point_grads[layer] = weight_grad(mixed[layer], grad_low)
        if layer == convs - 1:
            sent = [to_row(jnp.stack([point_grads[layer], point_grads[convs]]))]
        elif layer == 2:
            sent.append(to_row(jnp.stack([point_grads[2], point_grads[3]])))
    if parts == 1:
        in_pieces = with_permutes(list(result[2:]))
    else:
        in_pieces = [over_rows(result[2][:own].reshape(batches, frames, channels))]

    devices = across_dp * across_tm
    excite_low = (excite_grad.reshape(-1, channels) * (1.0 / parts)).astype(LOW)
    small = jnp.concatenate(small_grads + [excite_low], axis=0)
    small_rows = -(-small.shape[0] // devices)
    small = jnp.pad(small, ((0, small_rows * devices - small.shape[0]), (0, 0)))
    send = jnp.concatenate(
        [g.reshape(across_dp, -1, channels).astype(LOW) for g in point_grads[:2]]
        + [small.reshape(across_dp, -1, channels)],
        axis=1,
    )
    held = jnp.sum(exchange(send, "dp").astype(F32), axis=0)
    big = 2 * across_tm * shard_rows
    point_all = jnp.concatenate(
        [held[:big].reshape(2, across_tm, shard_rows, channels)]
        + [part.reshape(-1, across_tm, shard_rows, channels) for part in sent[::-1]],
        axis=0,
    ).astype(LOW)
    send = jnp.concatenate(
        [
            jnp.transpose(point_all, (1, 0, 2, 3)).reshape(across_tm, -1, channels),
            held[big:].reshape(across_tm, -1, channels).astype(LOW),
        ],
        axis=1,
    )
    send, in_pieces[1::2] = lax.optimization_barrier((send, in_pieces[1::2]))
    held = jnp.sum(exchange(send, "tm").astype(F32), axis=0)
    input_grad = settle(in_pieces).astype(F32)
    block_out = settle(out_pieces)
    point_shard = held[: matrices * shard_rows].reshape(pointwise.shape)
    small_shard = held[matrices * shard_rows :]

    pw_moment, pw_square, pw_update = lamb_terms(
        pointwise, pointwise_first, pointwise_second, point_shard
    )
    squares = jnp.concatenate(
        [
            jnp.sum(pointwise * pointwise, axis=(1, 2)),
            jnp.sum(pw_update * pw_update, axis=(1, 2)),
        ]
    )
    squares = three_parts(squares[None])
    squares = jnp.pad(squares, ((0, 0), (0, LANES - squares.shape[1]))).reshape(1, -1)
    squares = jnp.pad(squares, ((0, 0), (0, channels - squares.shape[1])))
    everything = exchange(
        copies_of(jnp.concatenate([small_shard.astype(LOW), squares], axis=0), devices),
        ("dp", "tm"),
    )
    if parts == 1:

        def turned(value):
            return jnp.transpose(value, (1, 0, 2))

        depth = [depthwise, depthwise_first, depthwise_second]
        norm = [turned(value) for value in (norm_affine, norm_first, norm_second)]
        excite = [excite_mats, excite_first, excite_second]
        tensors = depth + norm + excite
        everything = everything.reshape(-1, channels)
        shapes = [(pointwise.shape, F32), (pointwise.shape, LOW)]
        shapes += [(value.shape, F32) for value in tensors]
        count = matrices + 3 * convs + excite_mats.shape[0]
        result = pl.pallas_call(
            functools.partial(finish_kernel, small_rows),
            out_shape=[
                jax.ShapeDtypeStruct(shape, dtype) for shape, dtype in shapes + [((2, count), F32)]
            ],
            scratch_shapes=[
                pltpu.VMEM(everything.shape, F32),
                pltpu.VMEM((2 * excite_mats.shape[1], channels), F32),
            ],
            compiler_params=pltpu.CompilerParams(vmem_limit_bytes=SCOPED),
        )(close(everything), pointwise, pw_update, *tensors)
        pw_new, pw_half = result[:2]
        return (
            block_out[:, None],
            input_grad[:, None],
            pw_moment,
            pw_square,
            pw_new,
            pw_half,
            *result[2:5],
            *[turned(value) for value in result[5:8]],
            *result[8:11],
            result[11],
        )
    everything = everything.astype(F32)
    squares = jnp.sum(everything[:, small_rows].reshape(devices, -1, LANES), axis=(0, 1))
    small = everything[:, :small_rows].reshape(-1, channels)
    cut = convs * SEGROWS
    by_layer = small[:cut].reshape(convs, SEGROWS, channels)
    grad_depth = by_layer[:, :taps]
    grad_norm = jnp.transpose(by_layer[:, taps : taps + 2], (1, 0, 2))
    grad_excite = small[cut : cut + 2 * excite_mats.shape[1]].reshape(excite_mats.shape)
    pw_wn = jnp.sqrt(squares[:matrices])
    pw_un = jnp.sqrt(squares[matrices : 2 * matrices])
    pw_new = pointwise - RATE * (pw_wn / pw_un)[:, None, None] * pw_update
    dw_moment, dw_square, dw_new, dw_wn, dw_un = local_lamb(
        depthwise, depthwise_first, depthwise_second, grad_depth, (1, 2)
    )
    nm_moment, nm_square, nm_new, nm_wn, nm_un = local_lamb(
        norm_affine, norm_first, norm_second, grad_norm, (2,)
    )
    se_moment, se_square, se_new, se_wn, se_un = local_lamb(
        excite_mats, excite_first, excite_second, grad_excite, (1, 2)
    )
    trust_norms = jnp.stack(
        [
            jnp.concatenate([pw_wn, dw_wn, nm_wn, se_wn]),
            jnp.concatenate([pw_un, dw_un, nm_un, se_un]),
        ]
    )
    return (
        block_out[:, None],
        input_grad[:, None],
        pw_moment,
        pw_square,
        pw_new,
        pw_new.astype(LOW),
        dw_moment,
        dw_square,
        dw_new,
        nm_moment,
        nm_square,
        nm_new,
        se_moment,
        se_square,
        se_new,
        trust_norms,
    )


def solution(mesh):
    rows = P(None, "dp", "tm", None)
    shards = P(None, ("dp", "tm"), None)
    return jax.shard_map(
        local,
        mesh=mesh,
        in_specs=(rows, P(None, "dp", "tm"), rows, shards, shards, shards) + (P(),) * 9,
        out_specs=(rows, rows, shards, shards, shards, shards) + (P(),) * 10,
        check_vma=False,
    )
```

time: 1210 us -> 341 us (0.28); the launches traced: 1200 us -> 339 us
  blocking collectives: 481 us -> 45.1 us
  starting transfers between devices: 263 us -> 64.2 us
  other arithmetic: 169 us -> 16.8 us
  Pallas kernels: 0 us -> 113 us
  matrix products: 116 us -> 14.5 us
  local copies, waits for them, and re-layouts: 63 us -> 5.68 us
  waiting for transfers between devices: 80.3 us -> 65.8 us
    psum x13 -> x0, blocking collectives: 481 us -> none  [the longest x5 204 us: local(): lax.psum((first_sum, square_sum, jnp.sum(live_mask)), ('dp', 'tm'))]
    ppermute x88 -> x12, starting transfers between devices: 263 us -> 23.3 us  [to_next(): lax.ppermute(piece, 'tm', [(i, (i + step) % batches) for i in range(batch...]
    pallas_call x0 -> x12, Pallas kernels: none -> 113 us  [the longest x11 110 us: run(): pl.pallas_call(body, out_shape=[jax.ShapeDtypeStruct(shape, dtype) for sh...]
    dot_general x112 -> x6, matrix products: 116 us -> 14.5 us  [low_dot(): lax.dot_general(left, right, (dims, ((), ())), preferred_element_type=F32)]
    reduce_scatter x1 -> x2, waiting for transfers between devices: 73.7 us -> 0.04 us  [to_row(): return lax.psum_scatter(grads, 'dp', scatter_dimension=1, tiled=True)]
    all_to_all x0 -> x11, waiting for transfers between devices: none -> 64.4 us  [exchange(): return lax.all_to_all(blocks, axis, 0, 0)]
    convert_element_type x87 -> x7, other arithmetic: 66.8 us -> 2.72 us  [the longest x1 1.94 us: local(): input_grad = settle(in_pieces).astype(F32)]
    reduce_sum x27 -> x3, other arithmetic: 50.8 us -> 2.22 us  [the longest x1 1.97 us: local(): jnp.sum(pw_update * pw_update, axis=(1, 2))]
  transfers between devices with their start and end apart: 91 -> 26, of which waited for: 4 -> 12; matrix products, arithmetic and copies ran while one was open for 17% -> 9% of each run, Pallas kernels for 0% -> 24%
where the time goes in v1:
time: 341 us; the launch traced here: 339 us
  Pallas kernels  113 us (33%)
  waiting for transfers between devices  65.8 us (19%)
  starting transfers between devices  64.2 us (19%)
  blocking collectives  45.1 us (13%)
  other arithmetic  16.8 us (5%)
  matrix products  14.5 us (4%)
  between operations  14.5 us (4%)
  local copies, waits for them, and re-layouts  5.68 us (2%)
    pallas_call x11, Pallas kernels, run(): pl.pallas_call(body, out_shape=[jax.ShapeDtypeStruct(shape, dtype) for sh...  110 us
    all_to_all x11, waiting for transfers between devices, exchange(): return lax.all_to_all(blocks, axis, 0, 0)  64.4 us
    all_to_all x11, starting transfers between devices, exchange(): return lax.all_to_all(blocks, axis, 0, 0)  40.6 us
    all_to_all x3, blocking collectives, exchange(): return lax.all_to_all(blocks, axis, 0, 0)  23.4 us
    ppermute x12, starting transfers between devices, to_next(): lax.ppermute(piece, 'tm', [(i, (i + step) % batches) for i in range(batch...  23.3 us
    dot_general x6, matrix products, low_dot(): lax.dot_general(left, right, (dims, ((), ())), preferred_element_type=F32)  14.5 us
    all_gather x1, blocking collectives, local(): early[0] = lax.all_gather(early[0], 'dp', tiled=True)  10.9 us
    all_gather x1, blocking collectives, local(): early[1] = lax.all_gather(early[1], 'dp', tiled=True)  10.7 us
  transfers between devices with their start and end apart: 26, of which 12 were waited for; matrix products, arithmetic and copies ran while one was open for 9% of the time, Pallas kernels for 24%

profile of v1, /device:TPU:0, one launch (start us, length us, event | category | flops | bytes accessed | tf_op | source)
XLA Modules:
  0.0 339.2 jit_solution(14916436483173673284)
XLA Ops:
  10.6 6.3 %all-to-all-start = ((bf16[4,33,512]{2,1,0:T(8,128)(2,1)}), bf16[4,33,512]{2,1,0:T(8,128)(2,1)S(1)}, u32[]{:S(2)}, u32[]{:S(2)}) async-start(bf16[4,33,512]{2,1,0:T(8,128)(2,1)} %pad_maximum_fusion.4), calls=%async_computation | async-start | bytes 327680 | tf_op jit(solution)/shard_map/all_to_all | solution.py:884
  20.0 7.9 %all-to-all-done = bf16[4,33,512]{2,1,0:T(8,128)(2,1)S(1)} async-done(((bf16[4,33,512]{2,1,0:T(8,128)(2,1)}), bf16[4,33,512]{2,1,0:T(8,128)(2,1)S(1)}, u32[]{:S(2)}, u32[]{:S(2)}) %all-to-all-start) | async-done | bytes 135200 | tf_op jit(solution)/shard_map/all_to_all | solution.py:884
  28.7 10.9 %all_gather.9.rest_5_.rest_4_ = bf16[512,512]{1,0:T(8,128)(2,1)} all-gather(bf16[64,512]{1,0:T(8,128)(2,1)S(1)} %bitcast.109), channel_id=1, replica_groups=mesh['dp'=8,'tm'=4] {'dp'}, dimensions={0}, use_global_device_ids=true | all-gather | bytes 589824 | tf_op jit(solution)/shard_map/all_gather | solution.py:1106
  40.8 10.7 %all_gather.10.matrix_ref.rest_4_ = bf16[512,512]{1,0:T(8,128)(2,1)} all-gather(bf16[64,512]{1,0:T(8,128)(2,1)S(1)} %bitcast.108), channel_id=1, replica_groups=mesh['dp'=8,'tm'=4] {'dp'}, dimensions={0}, use_global_device_ids=true | all-gather | bytes 589824 | tf_op jit(solution)/shard_map/all_gather | solution.py:1108
  51.6 7.5 %shard_map.270 = (bf16[1536,512]{1,0:T(8,128)(2,1)}, f32[1536,512]{1,0:T(8,128)}, bf16[1536,512]{1,0:T(8,128)(2,1)}, f32[8,16,128]{2,1,0:T(8,128)}) custom-call(s32[1]{0:T(128)} %bitcast.me_ref, bf16[384,512]{1,0:T(8,128)(2,1)S(1)} %get-tuple-element.104.rest_0_, bf16[384,512]{1,0:T(8,128)(2,1)S(1)} %collective-permute-done.rest_1_, ...), custom_call_target="tpu_custom_call" | custom-call | flops 805306368 | bytes 2951168 | tf_op jit(solution)/shard_map/pallas_call | solution.py:866
  59.1 3.4 all-to-all-start.1
  63.1 4.3 %all-to-all-done.1.sums_ref = f32[8,16,128]{2,1,0:T(8,128)S(1)} async-done(((f32[8,16,128]{2,1,0:T(8,128)}), f32[8,16,128]{2,1,0:T(8,128)S(1)}, u32[]{:S(2)}, u32[]{:S(2)}) %all-to-all-start.1) | async-done | bytes 65568 | tf_op jit(solution)/shard_map/all_to_all | solution.py:884
  67.5 6.9 %shard_map.271 = (bf16[1536,512]{1,0:T(8,128)(2,1)}, f32[1536,512]{1,0:T(8,128)}, f32[8,8,128]{2,1,0:T(8,128)}, f32[8,512]{1,0:T(8,128)}, f32[8,128]{1,0:T(8,128)}) custom-call(f32[1568,128]{1,0:T(8,128)} %broadcast_in_dim.28.rest_4_.codes_ref.rest_0_, f32[1536,512]{1,0:T(8,128)} %get-tuple-element.106.before_ref.rest_3_.rest_2_, ...), custom_call_target="tpu_custom_call" | custom-call | flops 805306368 | bytes 4610048 | tf_op jit(solution)/shard_map/pallas_call | solution.py:866
  74.5 9.6 %collective-permute-start.3 = (bf16[384,512]{1,0:T(8,128)(2,1)S(1)}, bf16[384,512]{1,0:T(8,128)(2,1)S(1)}, u32[]{:S(2)}, u32[]{:S(2)}) collective-permute-start(bf16[384,512]{1,0:T(8,128)(2,1)S(1)} %get-tuple-element.278), channel_id=1, source_target_pairs={{0,1},{1,2},{2,3},{3,0},{4,5},{5,6},{6,7},{7,4},{8,9},{9,10},{10,1... | collective-permute-start | bytes 1179656 | tf_op jit(solution)/shard_map/ppermute | solution.py:1022
  86.5 7.2 %all_to_all.70.sums_ref = f32[8,8,128]{2,1,0:T(8,128)S(1)} all-to-all(f32[8,8,128]{2,1,0:T(8,128)S(1)} %copy-done.16), channel_id=1, replica_groups=mesh['dp'=8,'tm'=4] {'dp'}, dimensions={0} | all-to-all | bytes 65536 | tf_op jit(solution)/shard_map/all_to_all | solution.py:884
  93.8 6.8 %shard_map.272 = (bf16[1536,512]{1,0:T(8,128)(2,1)}, f32[1536,512]{1,0:T(8,128)}, f32[8,8,128]{2,1,0:T(8,128)}, f32[8,512]{1,0:T(8,128)}) custom-call(f32[1568,128]{1,0:T(8,128)} %broadcast_in_dim.28.rest_4_.codes_ref.rest_0_, f32[1536,512]{1,0:T(8,128)} %get-tuple-element.111.before_ref.rest_3_.rest_2_, ...), custom_call_target="tpu_custom_call" | custom-call | flops 805306368 | bytes 6154240 | tf_op jit(solution)/shard_map/pallas_call | solution.py:866
  100.5 8.1 %all_to_all.71.sums_ref = f32[8,8,128]{2,1,0:T(8,128)S(1)} all-to-all(f32[8,8,128]{2,1,0:T(8,128)} %get-tuple-element.115), channel_id=1, replica_groups=mesh['dp'=8,'tm'=4] {'dp'}, dimensions={0} | all-to-all | bytes 65536 | tf_op jit(solution)/shard_map/all_to_all | solution.py:884
  108.6 6.8 %shard_map.273 = (bf16[1536,512]{1,0:T(8,128)(2,1)}, f32[1536,512]{1,0:T(8,128)}, f32[8,8,128]{2,1,0:T(8,128)}, f32[8,512]{1,0:T(8,128)}) custom-call(f32[1568,128]{1,0:T(8,128)} %broadcast_in_dim.28.rest_4_.codes_ref.rest_0_, f32[1536,512]{1,0:T(8,128)} %get-tuple-element.114.before_ref.rest_3_.rest_2_, ...), custom_call_target="tpu_custom_call" | custom-call | flops 805306368 | bytes 6154240 | tf_op jit(solution)/shard_map/pallas_call | solution.py:866
  115.4 8.1 %all_to_all.72.sums_ref = f32[8,8,128]{2,1,0:T(8,128)S(1)} all-to-all(f32[8,8,128]{2,1,0:T(8,128)} %get-tuple-element.117), channel_id=1, replica_groups=mesh['dp'=8,'tm'=4] {'dp'}, dimensions={0} | all-to-all | bytes 65536 | tf_op jit(solution)/shard_map/all_to_all | solution.py:884
  123.5 6.8 %shard_map.274 = (bf16[1536,512]{1,0:T(8,128)(2,1)}, f32[1536,512]{1,0:T(8,128)}, f32[8,8,128]{2,1,0:T(8,128)}, f32[8,512]{1,0:T(8,128)}) custom-call(f32[1568,128]{1,0:T(8,128)} %broadcast_in_dim.28.rest_4_.codes_ref.rest_0_, f32[1536,512]{1,0:T(8,128)} %get-tuple-element.116.before_ref.rest_3_.rest_2_, ...), custom_call_target="tpu_custom_call" | custom-call | flops 805306368 | bytes 6154240 | tf_op jit(solution)/shard_map/pallas_call | solution.py:866
  130.3 3.4 all-to-all-start.5
  134.4 4.1 %all-to-all-done.5.rest_8_ = f32[8,8,128]{2,1,0:T(8,128)S(1)} async-done(((f32[8,8,128]{2,1,0:T(8,128)}), f32[8,8,128]{2,1,0:T(8,128)S(1)}, u32[]{:S(2)}, u32[]{:S(2)}) %all-to-all-start.5) | async-done | bytes 32800 | tf_op jit(solution)/shard_map/all_to_all | solution.py:884
  138.4 15.4 %shard_map.275 = (bf16[384,512]{1,0:T(8,128)(2,1)}, bf16[384,512]{1,0:T(8,128)(2,1)}, bf16[384,512]{1,0:T(8,128)(2,1)}, bf16[384,512]{1,0:T(8,128)(2,1)}, bf16[1...) custom-call(s32[1]{0:T(128)} %bitcast.me_ref, ...), custom_call_target="tpu_custom_call" | custom-call | flops 805306368 | bytes 9379840 | tf_op jit(solution)/shard_map/pallas_call | solution.py:866
  153.8 3.4 all-to-all-start.6
  162.0 11.7 %shard_map.276 = (bf16[1536,512]{1,0:T(8,128)(2,1)}, bf16[16,512]{1,0:T(8,128)(2,1)}, f32[1536,512]{1,0:T(8,128)}, f32[8,8,128]{2,1,0:T(8,128)}) custom-call(s32[1]{0:T(128)} %bitcast.me_ref, f32[1568,128]{1,0:T(8,128)} %broadcast_in_dim.28.rest_4_.codes_ref.rest_0_, f32[1536,512]{1,0:T(8,128)} %get-tuple-element.121.rest_1_, ...), custom_call_target="tpu_custom_call" | custom-call | flops 1610612736 | bytes 12478464 | tf_op jit(solution)/shard_map/pallas_call | solution.py:866
  177.2 3.4 all-to-all-start.7
  185.3 11.8 %shard_map.277 = (bf16[1536,512]{1,0:T(8,128)(2,1)}, bf16[16,512]{1,0:T(8,128)(2,1)}, f32[1536,512]{1,0:T(8,128)}, f32[8,8,128]{2,1,0:T(8,128)}) custom-call(s32[1]{0:T(128)} %bitcast.me_ref, f32[1568,128]{1,0:T(8,128)} %broadcast_in_dim.28.rest_4_.codes_ref.rest_0_, f32[1536,512]{1,0:T(8,128)} %get-tuple-element.125.rest_1_, ...), custom_call_target="tpu_custom_call" | custom-call | flops 1610612736 | bytes 12478464 | tf_op jit(solution)/shard_map/pallas_call | solution.py:866
  197.1 3.4 all-to-all-start.8
  205.2 11.8 %shard_map.278 = (bf16[1536,512]{1,0:T(8,128)(2,1)}, bf16[16,512]{1,0:T(8,128)(2,1)}, f32[1536,512]{1,0:T(8,128)}, f32[8,8,128]{2,1,0:T(8,128)}) custom-call(s32[1]{0:T(128)} %bitcast.me_ref, f32[1568,128]{1,0:T(8,128)} %broadcast_in_dim.28.rest_4_.codes_ref.rest_0_, f32[1536,512]{1,0:T(8,128)} %get-tuple-element.128.rest_1_, ...), custom_call_target="tpu_custom_call" | custom-call | flops 1610612736 | bytes 12478464 | tf_op jit(solution)/shard_map/pallas_call | solution.py:866
  225.2 11.6 %shard_map.279 = (bf16[1536,512]{1,0:T(8,128)(2,1)}, bf16[16,512]{1,0:T(8,128)(2,1)}, f32[1536,512]{1,0:T(8,128)}, f32[8,8,128]{2,1,0:T(8,128)}) custom-call(s32[1]{0:T(128)} %bitcast.me_ref, f32[1568,128]{1,0:T(8,128)} %broadcast_in_dim.28.rest_4_.codes_ref.rest_0_, f32[1536,512]{1,0:T(8,128)} %get-tuple-element.133.rest_1_, ...), custom_call_target="tpu_custom_call" | custom-call | flops 1610612736 | bytes 10905600 | tf_op jit(solution)/shard_map/pallas_call | solution.py:866
  245.0 12.8 %shard_map.280 = (bf16[1536,512]{1,0:T(8,128)(2,1)}, bf16[16,512]{1,0:T(8,128)(2,1)}, bf16[384,512]{1,0:T(8,128)(2,1)}, bf16[384,512]{1,0:T(8,128)(2,1)}, bf16[3...) custom-call(s32[1]{0:T(128)} %bitcast.me_ref, f32[1568,128]{1,0:T(8,128)} %broadcast_in_dim.28.rest_4_.codes_ref.rest_0_, ...), custom_call_target="tpu_custom_call" | custom-call | flops 1610612736 | bytes 12986368 | tf_op jit(solution)/shard_map/pallas_call | solution.py:866
  262.3 3.6 %all-to-all-start.11 = ((bf16[8,156,512]{2,1,0:T(8,128)(2,1)}), bf16[8,156,512]{2,1,0:T(8,128)(2,1)S(1)}, u32[]{:S(2)}, u32[]{:S(2)}) async-start(bf16[8,156,512]{2,1,0:T(8,128)(2,1)} %pad_maximum_fusion), calls=%async_computation.11 | async-start | bytes 2621440 | tf_op jit(solution)/shard_map/all_to_all | solution.py:884
  268.2 15.9 %all-to-all-done.11 = bf16[8,156,512]{2,1,0:T(8,128)(2,1)S(1)} async-done(((bf16[8,156,512]{2,1,0:T(8,128)(2,1)}), bf16[8,156,512]{2,1,0:T(8,128)(2,1)S(1)}, u32[]{:S(2)}, u32[]{:S(2)}) %all-to-all-start.11) | async-done | bytes 1277984 | tf_op jit(solution)/shard_map/all_to_all | solution.py:884
  287.6 3.5 %all-to-all-start.12 = ((bf16[4,103,512]{2,1,0:T(8,128)(2,1)}), bf16[4,103,512]{2,1,0:T(8,128)(2,1)S(1)}, u32[]{:S(2)}, u32[]{:S(2)}) async-start(bf16[4,103,512]{2,1,0:T(8,128)(2,1)} %pad_maximum_fusion.3), calls=%async_computation.14 | async-start | bytes 851968 | tf_op jit(solution)/shard_map/all_to_all | solution.py:884
  295.2 17.7 %all-to-all-done.12 = bf16[4,103,512]{2,1,0:T(8,128)(2,1)S(1)} async-done(((bf16[4,103,512]{2,1,0:T(8,128)(2,1)}), bf16[4,103,512]{2,1,0:T(8,128)(2,1)S(1)}, u32[]{:S(2)}, u32[]{:S(2)}) %all-to-all-start.12) | async-done | bytes 421920 | tf_op jit(solution)/shard_map/all_to_all | solution.py:884
  315.8 3.8 %all-to-all-start.13 = ((bf16[32,8,512]{2,1,0:T(8,128)(2,1)}), bf16[32,8,512]{2,1,0:T(8,128)(2,1)S(1)}, u32[]{:S(2)}, u32[]{:S(2)}) async-start(bf16[32,8,512]{2,1,0:T(8,128)(2,1)} %broadcast_in_dim.30), calls=%async_computation.15 | async-start | bytes 524288 | tf_op jit(solution)/shard_map/all_to_all | solution.py:884
  324.2 5.6 %all-to-all-done.13 = bf16[32,8,512]{2,1,0:T(8,128)(2,1)S(1)} async-done(((bf16[32,8,512]{2,1,0:T(8,128)(2,1)}), bf16[32,8,512]{2,1,0:T(8,128)(2,1)S(1)}, u32[]{:S(2)}, u32[]{:S(2)}) %all-to-all-start.13) | async-done | bytes 262176 | tf_op jit(solution)/shard_map/all_to_all | solution.py:884
  (148 shorter events, 70.9 us)
Async XLA Ops:
  7.2 21.2 %copy-start.7 = (bf16[4,1,384,512]{3,2,1,0:T(8,128)(2,1)S(1)}, bf16[4,1,384,512]{3,2,1,0:T(8,128)(2,1)}, u32[]{:S(2)}) copy-start(bf16[4,1,384,512]{3,2,1,0:T(8,128)(2,1)} %param.15) | copy-start | bytes 4718596
  7.2 86.6 %all-gather.2.cloned.1.call-start = ((), (), s32[]{:S(2)}) async-start(), calls=%async_computation.16 | async-start | bytes 2162688 | tf_op jit(solution)/shard_map/all_gather | solution.py:1086
  10.6 17.4 %all-to-all-start = ((bf16[4,33,512]{2,1,0:T(8,128)(2,1)}), bf16[4,33,512]{2,1,0:T(8,128)(2,1)S(1)}, u32[]{:S(2)}, u32[]{:S(2)}) async-start(bf16[4,33,512]{2,1,0:T(8,128)(2,1)} %pad_maximum_fusion.4), calls=%async_computation | async-start | bytes 327680 | tf_op jit(solution)/shard_map/all_to_all | solution.py:884
  18.0 33.6 %collective-permute-start = (bf16[384,512]{1,0:T(8,128)(2,1)S(1)}, bf16[384,512]{1,0:T(8,128)(2,1)S(1)}, u32[]{:S(2)}, u32[]{:S(2)}) collective-permute-start(bf16[384,512]{1,0:T(8,128)(2,1)S(1)} %dynamic-slice_bitcast_fusion.6), channel_id=1, source_target_pairs={{0,1},{1,2},{2,3},{3,0},{4,5},{5,6},{6,7},{7,4},{8,9},{9,10},{10,1... | collective-permute-start | bytes 1179656 | tf_op jit(solution)/shard_map/ppermute | solution.py:1022
  28.5 23.1 %collective-permute-start.1 = (bf16[384,512]{1,0:T(8,128)(2,1)S(1)}, bf16[384,512]{1,0:T(8,128)(2,1)S(1)}, u32[]{:S(2)}, u32[]{:S(2)}) collective-permute-start(bf16[384,512]{1,0:T(8,128)(2,1)S(1)} %get-tuple-element.281), channel_id=1, source_target_pairs={{0,2},{1,3},{2,0},{3,1},{4,6},{5,7},{6,4},{7,5},{8,10},{9,11},{10,... | collective-permute-start | bytes 1179656 | tf_op jit(solution)/shard_map/ppermute | solution.py:1022
  28.6 23.0 %collective-permute-start.2 = (bf16[384,512]{1,0:T(8,128)(2,1)S(1)}, bf16[384,512]{1,0:T(8,128)(2,1)S(1)}, u32[]{:S(2)}, u32[]{:S(2)}) collective-permute-start(bf16[384,512]{1,0:T(8,128)(2,1)S(1)} %get-tuple-element.280), channel_id=1, source_target_pairs={{0,3},{1,0},{2,1},{3,2},{4,7},{5,4},{6,5},{7,6},{8,11},{9,8},{10,9... | collective-permute-start | bytes 1179656 | tf_op jit(solution)/shard_map/ppermute | solution.py:1022
  59.1 8.3 %all-to-all-start.1 = ((f32[8,16,128]{2,1,0:T(8,128)}), f32[8,16,128]{2,1,0:T(8,128)S(1)}, u32[]{:S(2)}, u32[]{:S(2)}) async-start(f32[8,16,128]{2,1,0:T(8,128)} %get-tuple-element.108), calls=%async_computation.1 | async-start | bytes 131072 | tf_op jit(solution)/shard_map/all_to_all | solution.py:884
  74.5 59.9 %collective-permute-start.3 = (bf16[384,512]{1,0:T(8,128)(2,1)S(1)}, bf16[384,512]{1,0:T(8,128)(2,1)S(1)}, u32[]{:S(2)}, u32[]{:S(2)}) collective-permute-start(bf16[384,512]{1,0:T(8,128)(2,1)S(1)} %get-tuple-element.278), channel_id=1, source_target_pairs={{0,1},{1,2},{2,3},{3,0},{4,5},{5,6},{6,7},{7,4},{8,9},{9,10},{10,1... | collective-permute-start | bytes 1179656 | tf_op jit(solution)/shard_map/ppermute | solution.py:1022
  84.1 50.3 %collective-permute-start.4 = (bf16[384,512]{1,0:T(8,128)(2,1)S(1)}, bf16[384,512]{1,0:T(8,128)(2,1)S(1)}, u32[]{:S(2)}, u32[]{:S(2)}) collective-permute-start(bf16[384,512]{1,0:T(8,128)(2,1)S(1)} %get-tuple-element.277), channel_id=1, source_target_pairs={{0,2},{1,3},{2,0},{3,1},{4,6},{5,7},{6,4},{7,5},{8,10},{9,11},{10,... | collective-permute-start | bytes 1179656 | tf_op jit(solution)/shard_map/ppermute | solution.py:1022
  85.0 49.3 %collective-permute-start.5 = (bf16[384,512]{1,0:T(8,128)(2,1)S(1)}, bf16[384,512]{1,0:T(8,128)(2,1)S(1)}, u32[]{:S(2)}, u32[]{:S(2)}) collective-permute-start(bf16[384,512]{1,0:T(8,128)(2,1)S(1)} %get-tuple-element.276), channel_id=1, source_target_pairs={{0,3},{1,0},{2,1},{3,2},{4,7},{5,4},{6,5},{7,6},{8,11},{9,8},{10,9... | collective-permute-start | bytes 1179656 | tf_op jit(solution)/shard_map/ppermute | solution.py:1022
  130.3 8.1 %all-to-all-start.5 = ((f32[8,8,128]{2,1,0:T(8,128)}), f32[8,8,128]{2,1,0:T(8,128)S(1)}, u32[]{:S(2)}, u32[]{:S(2)}) async-start(f32[8,8,128]{2,1,0:T(8,128)} %get-tuple-element.120), calls=%async_computation.5 | async-start | bytes 65536 | tf_op jit(solution)/shard_map/all_to_all | solution.py:884
  138.4 19.0 %copy-start = (bf16[1536,512]{1,0:T(8,128)(2,1)S(1)}, bf16[1536,512]{1,0:T(8,128)(2,1)}, u32[]{:S(2)}) copy-start(bf16[1536,512]{1,0:T(8,128)(2,1)} %get-tuple-element.119.rest_6_.rest_3_) | copy-start | bytes 4718596
  153.8 8.1 %all-to-all-start.6 = ((f32[8,8,128]{2,1,0:T(8,128)}), f32[8,8,128]{2,1,0:T(8,128)S(1)}, u32[]{:S(2)}, u32[]{:S(2)}) async-start(f32[8,8,128]{2,1,0:T(8,128)} %get-tuple-element.122), calls=%async_computation.6 | async-start | bytes 65536 | tf_op jit(solution)/shard_map/all_to_all | solution.py:884
  157.2 127.1 %reduce-scatter.5.cloned.1.call-start = ((), (), s32[]{:S(2)}) async-start(), calls=%async_computation.18 | async-start | bytes 1179648 | tf_op jit(solution)/shard_map/reduce_scatter | solution.py:1260
  177.2 8.1 %all-to-all-start.7 = ((f32[8,8,128]{2,1,0:T(8,128)}), f32[8,8,128]{2,1,0:T(8,128)S(1)}, u32[]{:S(2)}, u32[]{:S(2)}) async-start(f32[8,8,128]{2,1,0:T(8,128)} %get-tuple-element.126), calls=%async_computation.7 | async-start | bytes 65536 | tf_op jit(solution)/shard_map/all_to_all | solution.py:884
  180.5 24.7 %collective-permute-start.6 = (bf16[384,512]{1,0:T(8,128)(2,1)}, bf16[384,512]{1,0:T(8,128)(2,1)S(1)}, u32[]{:S(2)}, u32[]{:S(2)}) collective-permute-start(bf16[384,512]{1,0:T(8,128)(2,1)} %get-tuple-element.130), channel_id=1, source_target_pairs={{0,1},{1,2},{2,3},{3,0},{4,5},{5,6},{6,7},{7,4},{8,9},{9,10},{10,1... | collective-permute-start | bytes 1179656 | tf_op jit(solution)/shard_map/ppermute | solution.py:1022
  181.1 42.9 %collective-permute-start.7 = (bf16[384,512]{1,0:T(8,128)(2,1)}, bf16[384,512]{1,0:T(8,128)(2,1)S(1)}, u32[]{:S(2)}, u32[]{:S(2)}) collective-permute-start(bf16[384,512]{1,0:T(8,128)(2,1)} %get-tuple-element.135), channel_id=1, source_target_pairs={{0,2},{1,3},{2,0},{3,1},{4,6},{5,7},{6,4},{7,5},{8,10},{9,11},{10,... | collective-permute-start | bytes 1179656 | tf_op jit(solution)/shard_map/ppermute | solution.py:1022
  183.1 59.5 %collective-permute-start.8 = (bf16[384,512]{1,0:T(8,128)(2,1)}, bf16[384,512]{1,0:T(8,128)(2,1)}, u32[]{:S(2)}, u32[]{:S(2)}) collective-permute-start(bf16[384,512]{1,0:T(8,128)(2,1)} %get-tuple-element.139), channel_id=1, source_target_pairs={{0,3},{1,0},{2,1},{3,2},{4,7},{5,4},{6,5},{7,6},{8,11},{9,8},{10,9... | collective-permute-start | bytes 1179656 | tf_op jit(solution)/shard_map/ppermute | solution.py:1022
  185.3 15.1 %copy-start.5 = (bf16[1536,512]{1,0:T(8,128)(2,1)S(1)}, bf16[1536,512]{1,0:T(8,128)(2,1)}, u32[]{:S(2)}) copy-start(bf16[1536,512]{1,0:T(8,128)(2,1)} %get-tuple-element.159) | copy-start | bytes 4718596
  197.1 8.2 %all-to-all-start.8 = ((f32[8,8,128]{2,1,0:T(8,128)}), f32[8,8,128]{2,1,0:T(8,128)S(1)}, u32[]{:S(2)}, u32[]{:S(2)}) async-start(f32[8,8,128]{2,1,0:T(8,128)} %get-tuple-element.129), calls=%async_computation.8 | async-start | bytes 65536 | tf_op jit(solution)/shard_map/all_to_all | solution.py:884
  205.2 15.2 %copy-start.4 = (bf16[1536,512]{1,0:T(8,128)(2,1)S(1)}, bf16[1536,512]{1,0:T(8,128)(2,1)}, u32[]{:S(2)}) copy-start(bf16[1536,512]{1,0:T(8,128)(2,1)} %get-tuple-element.157) | copy-start | bytes 4718596
  217.0 8.1 %all-to-all-start.9 = ((f32[8,8,128]{2,1,0:T(8,128)}), f32[8,8,128]{2,1,0:T(8,128)S(1)}, u32[]{:S(2)}, u32[]{:S(2)}) async-start(f32[8,8,128]{2,1,0:T(8,128)} %get-tuple-element.134), calls=%async_computation.9 | async-start | bytes 65536 | tf_op jit(solution)/shard_map/all_to_all | solution.py:884
  220.4 64.0 %reduce-scatter.3.cloned.1.call-start = ((), (), s32[]{:S(2)}) async-start(), calls=%async_computation.17 | async-start | bytes 1179648 | tf_op jit(solution)/shard_map/reduce_scatter | solution.py:1260
  225.2 15.0 %copy-start.3 = (bf16[1536,512]{1,0:T(8,128)(2,1)S(1)}, bf16[1536,512]{1,0:T(8,128)(2,1)}, u32[]{:S(2)}) copy-start(bf16[1536,512]{1,0:T(8,128)(2,1)} %get-tuple-element.149) | copy-start | bytes 4718596
  236.8 8.1 %all-to-all-start.10 = ((f32[8,8,128]{2,1,0:T(8,128)}), f32[8,8,128]{2,1,0:T(8,128)S(1)}, u32[]{:S(2)}, u32[]{:S(2)}) async-start(f32[8,8,128]{2,1,0:T(8,128)} %get-tuple-element.138), calls=%async_computation.10 | async-start | bytes 65536 | tf_op jit(solution)/shard_map/all_to_all | solution.py:884
  262.3 21.7 %all-to-all-start.11 = ((bf16[8,156,512]{2,1,0:T(8,128)(2,1)}), bf16[8,156,512]{2,1,0:T(8,128)(2,1)S(1)}, u32[]{:S(2)}, u32[]{:S(2)}) async-start(bf16[8,156,512]{2,1,0:T(8,128)(2,1)} %pad_maximum_fusion), calls=%async_computation.11 | async-start | bytes 2621440 | tf_op jit(solution)/shard_map/all_to_all | solution.py:884
  265.9 20.4 %collective-permute-start.10 = (bf16[384,512]{1,0:T(8,128)(2,1)}, bf16[384,512]{1,0:T(8,128)(2,1)S(1)}, u32[]{:S(2)}, u32[]{:S(2)}) collective-permute-start(bf16[384,512]{1,0:T(8,128)(2,1)} %get-tuple-element.164), channel_id=1, source_target_pairs={{0,3},{1,0},{2,1},{3,2},{4,7},{5,4},{6,5},{7,6},{8,11},{9,8},{10,9... | collective-permute-start | bytes 1179656 | tf_op jit(solution)/shard_map/ppermute | solution.py:1022
  268.2 19.4 %collective-permute-start.9 = (bf16[384,512]{1,0:T(8,128)(2,1)}, bf16[384,512]{1,0:T(8,128)(2,1)}, u32[]{:S(2)}, u32[]{:S(2)}) collective-permute-start(bf16[384,512]{1,0:T(8,128)(2,1)} %get-tuple-element.163), channel_id=1, source_target_pairs={{0,1},{1,2},{2,3},{3,0},{4,5},{5,6},{6,7},{7,4},{8,9},{9,10},{10,1... | collective-permute-start | bytes 1179656 | tf_op jit(solution)/shard_map/ppermute | solution.py:1022
  287.6 25.3 %all-to-all-start.12 = ((bf16[4,103,512]{2,1,0:T(8,128)(2,1)}), bf16[4,103,512]{2,1,0:T(8,128)(2,1)S(1)}, u32[]{:S(2)}, u32[]{:S(2)}) async-start(bf16[4,103,512]{2,1,0:T(8,128)(2,1)} %pad_maximum_fusion.3), calls=%async_computation.14 | async-start | bytes 851968 | tf_op jit(solution)/shard_map/all_to_all | solution.py:884
  291.1 29.8 %collective-permute-start.11 = (bf16[384,512]{1,0:T(8,128)(2,1)}, bf16[384,512]{1,0:T(8,128)(2,1)}, u32[]{:S(2)}, u32[]{:S(2)}) collective-permute-start(bf16[384,512]{1,0:T(8,128)(2,1)} %get-tuple-element.166), channel_id=1, source_target_pairs={{0,2},{1,3},{2,0},{3,1},{4,6},{5,7},{6,4},{7,5},{8,10},{9,11},{10,... | collective-permute-start | bytes 1179656 | tf_op jit(solution)/shard_map/ppermute | solution.py:1022
  293.9 19.0 %copy-start.1 = (f32[6,16,512]{2,1,0:T(8,128)S(1)}, f32[6,16,512]{2,1,0:T(8,128)}, u32[]{:S(2)}) copy-start(f32[6,16,512]{2,1,0:T(8,128)} %refs_1_.1) | copy-start | bytes 589828
  315.8 14.0 %all-to-all-start.13 = ((bf16[32,8,512]{2,1,0:T(8,128)(2,1)}), bf16[32,8,512]{2,1,0:T(8,128)(2,1)S(1)}, u32[]{:S(2)}, u32[]{:S(2)}) async-start(bf16[32,8,512]{2,1,0:T(8,128)(2,1)} %broadcast_in_dim.30), calls=%async_computation.15 | async-start | bytes 524288 | tf_op jit(solution)/shard_map/all_to_all | solution.py:884
  (15 other events, 148.3 us)
Sparse Core Ops, SparseCore 0:
  11.6 74.5 all-gather.1
  177.3 33.7 reduce-scatter.4
  224.4 36.1 reduce-scatter.2
